TPU v7x, 256 devices: a whole 4x4x8 slice. The times are simulated.
256 devices in a mesh: dp: 8 (over y, core), seq: 4 (over z_lo), tensor: 8 (over x, z_hi).
Axes of the slice: x: 4, y: 4, z: 8 (z_hi: 2, z_lo: 4; z = z_hi * 4 + z_lo), core: 2. Of those that a mesh axis runs over, the one named last changes fastest.
Arguments:
- queries: bfloat16 [8, 1024, 64, 128], P('dp', 'seq', 'tensor'), may hold values from -100 to 100
- keys: bfloat16 [8, 1024, 8, 128], P('dp', 'seq', 'tensor'), may hold values from -5 to 5
- values: bfloat16 [8, 1024, 8, 128], P('dp', 'seq', 'tensor'), may hold values from -6 to 6
- segment_ids: int32 [8, 1024], P('dp', 'seq'), may hold values from 0 to 7, never falling along the last dimension, each value on 1 to 512 neighbouring positions
- codes: int32 [4096, 8192], P(('dp', 'seq'), 'tensor'), may hold values from 0 to 15
- zero_points: int32 [4096, 64], P(('dp', 'seq'), 'tensor'), may hold values from 4 to 11
- step_sizes: bfloat16 [4096, 64], P(('dp', 'seq'), 'tensor'), may hold values from 0.0009994507 to 0.0039978027
- cotangent: bfloat16 [8, 1024, 4096], P('dp', 'seq'), may hold values from -6 to 6
Outputs:
- grad_steps: float32 [4096, 64], P(('dp', 'seq'), 'tensor')
- grad_queries: bfloat16 [8, 1024, 64, 128], P('dp', 'seq', 'tensor')
- key_gradient: bfloat16 [8, 1024, 8, 128], P('dp', 'seq', 'tensor')
- value_gradient: bfloat16 [8, 1024, 8, 128], P('dp', 'seq', 'tensor')
Inputs may be any that keep to these rules, and one draw needn't show every extreme that they name: `segment_ids`: documents are runs of consecutive positions numbered from 0 upward.
All inputs are finite; a program needn't handle non-finite values.
Results may differ from a plain program's by a relative error of at most 0.035.
Values may be sent and summed in bfloat16 or wider, within the bound.
A program may use at most 128 MiB of HBM per device.

v0:
```python
import jax
import jax.numpy as jnp
from jax import lax
from jax.sharding import PartitionSpec as P

GROUP = 128


def local(queries, keys, values, segment_ids, codes, zero_points, step_sizes, cotangent):
    query_loc = queries[0]
    tok_rows = query_loc.shape[0]
    heads_loc = query_loc.shape[1]
    head_size = query_loc.shape[2]
    kv_heads = keys.shape[2]
    group_index = heads_loc // kv_heads
    features = heads_loc * head_size
    groups_loc = features // GROUP
    scale_factor = head_size ** (-0.5)
    seg_low = segment_ids.astype(jnp.bfloat16)
    whole_keys, whole_values, whole_seg = (
        lax.all_gather(keys, "seq", axis=1, tiled=True),
        lax.all_gather(values, "seq", axis=1, tiled=True),
        lax.all_gather(seg_low, "seq", axis=1, tiled=True),
    )
    key_all = whole_keys[0]
    value_all = whole_values[0]
    seg_all = whole_seg[0]
    length_count = key_all.shape[0]
    query_grp = query_loc.reshape(tok_rows, kv_heads, group_index, head_size)
    scores = (
        jnp.einsum("qcgd,kcd->cgqk", query_grp, key_all, preferred_element_type=jnp.float32)
        * scale_factor
    )
    query_pos = lax.axis_index("seq") * tok_rows + jnp.arange(tok_rows, dtype=jnp.int32)
    key_pos = jnp.arange(length_count, dtype=jnp.int32)
    allowed = (key_pos[None, :] <= query_pos[:, None]) & (seg_all[None, :] == seg_low[0][:, None])
    allowed = allowed[None, None]
    capped = jnp.where(allowed, scores, jnp.float32(-1e30))
    top = jnp.max(capped, axis=-1, keepdims=True)
    expo = jnp.where(allowed, jnp.exp(capped - top), jnp.float32(0.0))
    prob = expo / jnp.sum(expo, axis=-1, keepdims=True)
    attended = jnp.einsum("cgqk,kcd->qcgd", prob, value_all.astype(jnp.float32)).astype(
        jnp.bfloat16
    )
    flat = attended.reshape(tok_rows, features)
    upstream = cotangent[0]
    centered = codes - jnp.repeat(zero_points, GROUP, axis=1)
    rows_loc = codes.shape[0]
    total_tokens = lax.axis_size("dp") * lax.axis_size("seq") * tok_rows
    weight_loc = (
        centered.astype(jnp.float32) * jnp.repeat(step_sizes.astype(jnp.float32), GROUP, axis=1)
    ).astype(jnp.bfloat16)
    columns = upstream
    grad_acc = jnp.dot(
        columns,
        lax.all_gather(weight_loc, ("dp", "seq"), axis=0, tiled=True),
        preferred_element_type=jnp.float32,
    )
    columns = upstream
    summed = lax.psum_scatter(
        lax.dot_general(
            columns, flat, (((0,), (0,)), ((), ())), preferred_element_type=jnp.float32
        ),
        ("dp", "seq"),
        scatter_dimension=0,
        tiled=True,
    )
    partial_steps = (
        (summed * centered.astype(jnp.float32)).reshape(rows_loc, groups_loc, GROUP).sum(-1)
    )
    grad_steps = partial_steps * total_tokens ** (-0.5)
    grad_out = grad_acc.astype(jnp.bfloat16).reshape(tok_rows, kv_heads, group_index, head_size)
    delta = jnp.sum(grad_out.astype(jnp.float32) * attended.astype(jnp.float32), axis=-1)
    delta = jnp.transpose(delta, (1, 2, 0))
    probability_lower = prob.astype(jnp.bfloat16)
    grad_prob = jnp.einsum(
        "qcgd,kcd->cgqk", grad_out, value_all, preferred_element_type=jnp.float32
    )
    score_gradient = (prob * (grad_prob - delta[..., None])).astype(jnp.bfloat16)
    grad_query = (
        jnp.einsum("cgqk,kcd->qcgd", score_gradient, key_all, preferred_element_type=jnp.float32)
        * scale_factor
    )
    grad_queries = grad_query.astype(jnp.bfloat16).reshape(1, tok_rows, heads_loc, head_size)
    key_part = (
        jnp.einsum("cgqk,qcgd->kcd", score_gradient, query_grp, preferred_element_type=jnp.float32)
        * scale_factor
    )
    value_part = jnp.einsum(
        "cgqk,qcgd->kcd", probability_lower, grad_out, preferred_element_type=jnp.float32
    )
    key_value = lax.psum_scatter(
        jnp.concatenate([key_part, value_part], axis=-1), "seq", scatter_dimension=0, tiled=True
    )
    key_gradient = key_value[:, :, :head_size].astype(jnp.bfloat16)[None]
    value_gradient = key_value[:, :, head_size:].astype(jnp.bfloat16)[None]
    return (grad_steps, grad_queries, key_gradient, value_gradient)


def solution(mesh):
    in_specs = (
        P("dp", "seq", "tensor", None),
        P("dp", "seq", "tensor", None),
        P("dp", "seq", "tensor", None),
        P("dp", "seq"),
        P(("dp", "seq"), "tensor"),
        P(("dp", "seq"), "tensor"),
        P(("dp", "seq"), "tensor"),
        P("dp", "seq", None),
    )
    out_specs = (
        P(("dp", "seq"), "tensor"),
        P("dp", "seq", "tensor", None),
        P("dp", "seq", "tensor", None),
        P("dp", "seq", "tensor", None),
    )
    return jax.shard_map(local, mesh=mesh, in_specs=in_specs, out_specs=out_specs, check_vma=False)
```

profile of v0, /device:TPU:2, one launch (start us, length us, event | category | flops | bytes accessed | tf_op | source)
XLA Modules:
  0.0 545.6 jit_solution(13729536505119859955)
XLA Ops:
  8.1 1.2 copy.15
  9.3 1.5 fusion.31
  11.5 0.9 copy.13
  12.5 1.3 copy.21
  13.8 12.2 %all_gather.14 = bf16[1,1024]{1,0:T(2,128)(2,1)S(1)} all-gather(bf16[1,256]{1,0:T(2,128)(2,1)S(1)} %convert_element_type.69), channel_id=1, replica_groups=mesh['dp'=8,'seq'=4,'tensor'=8] {'seq'}, dimensions={1}, use_global_device_ids=true | all-gather | bytes 2560 | tf_op jit(solution)/shard_map/all_gather | solution.py:23
  26.0 15.4 %all_gather.17 = bf16[1,1024,1,128]{1,3,2,0:T(8,128)(2,1)} all-gather(bf16[1,256,1,128]{1,3,2,0:T(8,128)(2,1)S(1)} %copy.13), channel_id=1, replica_groups=mesh['dp'=8,'seq'=4,'tensor'=8] {'seq'}, dimensions={1}, use_global_device_ids=true | all-gather | bytes 327680 | tf_op jit(solution)/shard_map/all_gather | solution.py:22
  41.4 14.2 %all_gather.16 = bf16[1,1024,1,128]{3,1,2,0:T(8,128)(2,1)S(1)} all-gather(bf16[1,256,1,128]{3,1,2,0:T(8,128)(2,1)} %param.9), channel_id=1, replica_groups=mesh['dp'=8,'seq'=4,'tensor'=8] {'seq'}, dimensions={1}, use_global_device_ids=true | all-gather | bytes 327680 | tf_op jit(solution)/shard_map/all_gather | solution.py:21
  56.6 1.4 fusion.4
  58.1 3.2 copy-done.1
  61.3 2.0 fusion.6
  63.3 52.0 %all-gather.2.cloned.1.call-done = bf16[4096,1024]{0,1:T(8,128)(2,1)} async-done(((bf16[128,1024]{0,1:T(8,128)(2,1)}), bf16[4096,1024]{0,1:T(8,128)(2,1)}) %all-gather.2.cloned.1.call-update) | async-done | bytes 8388624 | tf_op jit(solution)/shard_map/all_gather | solution.py:56
  115.2 5.9 %fusion.16 = bf16[1024,256]{1,0:T(8,128)(2,1)S(1)} fusion(bf16[4096,1024]{0,1:T(8,128)(2,1)} %all-gather.2.cloned.1.call-done, bf16[1,256,4096]{2,1,0:T(8,128)(2,1)S(1)} %copy-done), kind=kOutput, calls=%fused_computation.19 | convolution fusion | flops 2147745792 | bytes 11010048 | tf_op jit(solution)/shard_map/dot_general | solution.py:54
  121.2 2.9 fusion.23
  124.0 3.4 fusion.29
  127.4 3.3 fusion.7
  130.8 1.5 fusion.28
  132.7 1.0 pad_maximum_fusion
  134.0 9.1 %convolution_bitcast_fusion = f32[4096,1024]{0,1:T(8,128)} fusion(bf16[256,1024]{0,1:T(8,128)(2,1)} %bitcast.153, bf16[1,256,4096]{2,1,0:T(8,128)(2,1)S(1)} %copy-done), kind=kOutput, calls=%fused_computation | convolution fusion | flops 2147483648 | bytes 19398656 | tf_op jit(solution)/shard_map/dot_general | solution.py:61
  144.1 3.6 fusion.26
  147.7 1.1 copy.23
  148.9 17.0 %reduce-scatter.5.cloned.1.call-done = f32[256,1,256]{0,2,1:T(8,128)} async-done(((f32[1024,1,256]{0,2,1:T(8,128)}), f32[256,1,256]{0,2,1:T(8,128)}) %reduce-scatter.5.cloned.1.call-update) | async-done | bytes 262160 | tf_op jit(solution)/shard_map/reduce_scatter | solution.py:92
  165.8 1.0 convert.5
  168.3 369.1 %reduce-scatter.3.cloned.1.call-done = f32[128,1024]{0,1:T(8,128)} async-done(((f32[4096,1024]{0,1:T(8,128)}), f32[128,1024]{0,1:T(8,128)}) %reduce-scatter.3.cloned.1.call-update) | async-done | bytes 524304 | tf_op jit(solution)/shard_map/reduce_scatter | solution.py:60
  537.4 1.1 bitcast_reduce_fusion
  (31 shorter events, 6.4 us)
Async XLA Ops:
  7.2 108.1 %copy-start = (bf16[1,256,4096]{2,1,0:T(8,128)(2,1)S(1)}, bf16[1,256,4096]{2,1,0:T(8,128)(2,1)}, u32[]{:S(2)}) copy-start(bf16[1,256,4096]{2,1,0:T(8,128)(2,1)} %param.15) | copy-start | bytes 6291460
  7.2 108.1 %all-gather.2.cloned.1.call-start = ((), (), s32[]{:S(2)}) async-start(), calls=%async_computation.3 | async-start | bytes 8650752 | tf_op jit(solution)/shard_map/all_gather | solution.py:56
  10.8 155.1 %reduce-scatter.5.cloned.1.call-start = ((), (), s32[]{:S(2)}) async-start(), calls=%async_computation.4 | async-start | bytes 1310720 | tf_op jit(solution)/shard_map/reduce_scatter | solution.py:92
  55.6 1.0 copy-start.3
  58.1 3.2 copy-start.1
  115.2 5.9 %copy-start.2 = (f32[1024,256,8]{1,0,2:T(8,128)S(1)}, f32[1024,256,8]{1,0,2:T(8,128)}, u32[]{:S(2)}) copy-start(f32[1024,256,8]{1,0,2:T(8,128)} %copy-done.1) | copy-start | bytes 25165828
  121.2 2.9 copy-start.5
  130.8 1.9 copy-start.7
  133.8 403.6 %reduce-scatter.3.cloned.1.call-start = ((), (), s32[]{:S(2)}) async-start(), calls=%async_computation.2 | async-start | bytes 17301504 | tf_op jit(solution)/shard_map/reduce_scatter | solution.py:60
  143.1 0.9 copy-start.4
  143.1 394.2 %copy-start.6 = (s32[128,8]{0,1:T(8,128)S(1)}, s32[128,8]{0,1:T(8,128)}, u32[]{:S(2)}) copy-start(s32[128,8]{0,1:T(8,128)} %param.13) | copy-start | bytes 12292
Sparse Core Ops, SparseCore 0:
  10.9 104.2 all-gather.1
  133.9 31.8 reduce-scatter.4
  168.5 368.7 reduce-scatter.2
where the time goes:
time: 546 us
  waiting for transfers between devices  438 us (80%)
  blocking collectives  41.8 us (8%)
  matrix products  31.1 us (6%)
  between operations  13.9 us (3%)
  local copies, waits for them, and re-layouts  10.7 us (2%)
  other arithmetic  9.73 us (2%)
    reduce_scatter x1, waiting for transfers between devices, local(): lax.psum_scatter(lax.dot_general(columns, flat, (((0,), (0,)), ((), ())),...  369 us
    all_gather x1, waiting for transfers between devices, local(): lax.all_gather(weight_loc, ('dp', 'seq'), axis=0, tiled=True)  52 us
    reduce_scatter x1, waiting for transfers between devices, local(): lax.psum_scatter(jnp.concatenate([key_part, value_part], axis=-1), 'seq',...  17 us
    all_gather x1, blocking collectives, local(): lax.all_gather(values, 'seq', axis=1, tiled=True)  15.4 us
    all_gather x1, blocking collectives, local(): lax.all_gather(keys, 'seq', axis=1, tiled=True)  14.2 us
    all_gather x1, blocking collectives, local(): lax.all_gather(seg_low, 'seq', axis=1, tiled=True)  12.2 us
  transfers between devices with their start and end apart: 3, of which 3 were waited for; matrix products, arithmetic and copies ran while one was open for 4% of the time, Pallas kernels for 0%

commit v1 on v0

--- a/solution.py
+++ b/solution.py
@@ -51,24 +51,16 @@
         centered.astype(jnp.float32) * jnp.repeat(step_sizes.astype(jnp.float32), GROUP, axis=1)
     ).astype(jnp.bfloat16)
     columns = upstream
-    grad_acc = jnp.dot(
-        columns,
-        lax.all_gather(weight_loc, ("dp", "seq"), axis=0, tiled=True),
-        preferred_element_type=jnp.float32,
-    )
-    columns = upstream
-    summed = lax.psum_scatter(
-        lax.dot_general(
-            columns, flat, (((0,), (0,)), ((), ())), preferred_element_type=jnp.float32
-        ),
-        ("dp", "seq"),
-        scatter_dimension=0,
-        tiled=True,
+    weight_all = lax.all_gather(weight_loc, ("dp", "seq"), axis=0, tiled=True)
+    grad_acc = jnp.dot(columns, weight_all, preferred_element_type=jnp.float32)
+    grad_weight = lax.dot_general(
+        columns, flat, (((0,), (0,)), ((), ())), preferred_element_type=jnp.float32
     )
     partial_steps = (
-        (summed * centered.astype(jnp.float32)).reshape(rows_loc, groups_loc, GROUP).sum(-1)
+        (grad_weight * weight_all.astype(jnp.float32)).reshape(-1, groups_loc, GROUP).sum(-1)
     )
-    grad_steps = partial_steps * total_tokens ** (-0.5)
+    summed = lax.psum_scatter(partial_steps, ("dp", "seq"), scatter_dimension=0, tiled=True)
+    grad_steps = summed * total_tokens ** (-0.5) / step_sizes.astype(jnp.float32)
     grad_out = grad_acc.astype(jnp.bfloat16).reshape(tok_rows, kv_heads, group_index, head_size)
     delta = jnp.sum(grad_out.astype(jnp.float32) * attended.astype(jnp.float32), axis=-1)
     delta = jnp.transpose(delta, (1, 2, 0))

time: 546 us -> 312 us (0.57)
  waiting for transfers between devices: 438 us -> 207 us
    reduce_scatter x1, waiting for transfers between devices: 369 us -> 125 us  [local(): lax.psum_scatter(partial_steps, ('dp', 'seq'), scatter_dimension=0, tiled...]
    reduce_scatter x1, waiting for transfers between devices: 17 us -> 30.1 us  [local(): lax.psum_scatter(jnp.concatenate([key_part, value_part], axis=-1), 'seq',...]
    dot_general x1, matrix products: 9.11 us -> 3.02 us  [local(): lax.dot_general(columns, flat, (((0,), (0,)), ((), ())), preferred_elemen...]
  transfers between devices with their start and end apart: 3 -> 3, of which waited for: 3 -> 3; matrix products, arithmetic and copies ran while one was open for 4% -> 9% of each run, Pallas kernels for 0% -> 0%
where the time goes in v1:
time: 312 us; the launch traced here: 311 us
  waiting for transfers between devices  207 us (66%)
  blocking collectives  41.2 us (13%)
  matrix products  28.7 us (9%)
  between operations  14 us (4%)
  local copies, waits for them, and re-layouts  9.92 us (3%)
  other arithmetic  9.14 us (3%)
    reduce_scatter x1, waiting for transfers between devices, local(): lax.psum_scatter(partial_steps, ('dp', 'seq'), scatter_dimension=0, tiled...  125 us
    all_gather x1, waiting for transfers between devices, local(): weight_all = lax.all_gather(weight_loc, ('dp', 'seq'), axis=0, tiled=True)  52.5 us
    reduce_scatter x1, waiting for transfers between devices, local(): lax.psum_scatter(jnp.concatenate([key_part, value_part], axis=-1), 'seq',...  30.1 us
    all_gather x1, blocking collectives, local(): lax.all_gather(values, 'seq', axis=1, tiled=True)  14.7 us
    all_gather x1, blocking collectives, local(): lax.all_gather(keys, 'seq', axis=1, tiled=True)  14.3 us
    all_gather x1, blocking collectives, local(): lax.all_gather(seg_low, 'seq', axis=1, tiled=True)  12.2 us
    unnamed x23, local copies, waits for them, and re-layouts  8.59 us
  transfers between devices with their start and end apart: 3, of which 3 were waited for; matrix products, arithmetic and copies ran while one was open for 9% of the time, Pallas kernels for 0%

profile of v1, /device:TPU:2, one launch (start us, length us, event | category | flops | bytes accessed | tf_op | source)
XLA Modules:
  0.0 310.7 jit_solution(1584654384545483626)
XLA Ops:
  7.2 1.4 copy.15
  9.3 1.5 fusion.31
  10.8 0.9 copy.13
  12.5 1.3 copy.21
  13.8 12.2 %all_gather.14 = bf16[1,1024]{1,0:T(2,128)(2,1)S(1)} all-gather(bf16[1,256]{1,0:T(2,128)(2,1)S(1)} %convert_element_type.72), channel_id=1, replica_groups=mesh['dp'=8,'seq'=4,'tensor'=8] {'seq'}, dimensions={1}, use_global_device_ids=true | all-gather | bytes 2560 | tf_op jit(solution)/shard_map/all_gather | solution.py:23
  26.0 14.7 %all_gather.17 = bf16[1,1024,1,128]{1,3,2,0:T(8,128)(2,1)S(1)} all-gather(bf16[1,256,1,128]{1,3,2,0:T(8,128)(2,1)S(1)} %copy.13), channel_id=1, replica_groups=mesh['dp'=8,'seq'=4,'tensor'=8] {'seq'}, dimensions={1}, use_global_device_ids=true | all-gather | bytes 327680 | tf_op jit(solution)/shard_map/all_gather | solution.py:22
  40.7 14.3 %all_gather.16 = bf16[1,1024,1,128]{3,1,2,0:T(8,128)(2,1)S(1)} all-gather(bf16[1,256,1,128]{3,1,2,0:T(8,128)(2,1)} %param.9), channel_id=1, replica_groups=mesh['dp'=8,'seq'=4,'tensor'=8] {'seq'}, dimensions={1}, use_global_device_ids=true | all-gather | bytes 327680 | tf_op jit(solution)/shard_map/all_gather | solution.py:21
  56.0 1.4 fusion.4
  57.4 3.2 %copy-done.1 = f32[1024,256,8]{1,0,2:T(8,128)} copy-done((f32[1024,256,8]{1,0,2:T(8,128)}, f32[1024,256,8]{1,0,2:T(8,128)S(1)}, u32[]{:S(2)}) %copy-start.1) | copy-done | bytes 8388632
  60.6 2.0 fusion.6
  62.6 52.5 %all-gather.2.cloned.1.call-done = bf16[4096,1024]{0,1:T(8,128)(2,1)} async-done(((bf16[128,1024]{0,1:T(8,128)(2,1)}), bf16[4096,1024]{0,1:T(8,128)(2,1)}) %all-gather.2.cloned.1.call-update) | async-done | bytes 8388624 | tf_op jit(solution)/shard_map/all_gather | solution.py:54
  115.1 5.9 %fusion.16 = bf16[1024,256]{1,0:T(8,128)(2,1)S(1)} fusion(bf16[4096,1024]{0,1:T(8,128)(2,1)} %all-gather.2.cloned.1.call-done, bf16[1,256,4096]{2,1,0:T(8,128)(2,1)S(1)} %copy-done), kind=kOutput, calls=%fused_computation.20 | convolution fusion | flops 2147745792 | bytes 11010048 | tf_op jit(solution)/shard_map/dot_general | solution.py:55
  121.0 2.7 fusion.29
  123.8 3.0 bitcast_reduce_fusion
  127.1 5.3 %fusion.23 = f32[1024,1,128]{0,2,1:T(8,128)S(1)} fusion(bf16[256,8,128]{0,2,1:T(8,128)(2,1)} %bitcast.155, f32[8,256]{1,0:T(8,128)S(1)} %fusion.6, f32[8,256]{1,0:T(8,128)S(1)} %get-tuple-element.10, f32[1024,256,8]{1,0,2:T(8,128)} %copy-done.1, pred[256,1024]{0,1:T(8,128)(4,1)S(1)} %fusion.30), kind=kOutput, calls=%fused_computation.23 | convolution fusion | flops 549453824 | bytes 9715712 | tf_op jit(solution)/shard_map/cgqk,qcgd->kcd/dot_general | solution.py:81
  132.4 5.5 %fusion.7 = bf16[8,256,1024]{1,2,0:T(8,128)(2,1)S(1)} fusion(f32[8,256]{1,0:T(8,128)S(1)} %bitcast.158, bf16[256,8,128]{0,2,1:T(8,128)(2,1)S(1)} %bitcast.156, f32[8,256]{1,0:T(8,128)S(1)} %fusion.6, f32[8,256]{1,0:T(8,128)S(1)} %get-tuple-element.10, f32[1024,256,8]{1,0,2:T(8,128)} %copy-done.1, pred[256,1024]{0,1:T(8,128)(4,1)S(1)} %fusion.30, ...), kind=kOutput, calls=%fused_computation.12 | convolution fusion | flops 553648128 | bytes 13656064 | tf_op jit(solution)/shard_map/qcgd,kcd->cgqk/dot_general | solution.py:68
  137.9 1.5 fusion.28
  139.8 1.1 pad_maximum_fusion
  140.9 3.5 %fusion.26 = bf16[1,256,8,128]{3,1,2,0:T(8,128)(2,1)S(1)} fusion(bf16[8,256,1024]{1,2,0:T(8,128)(2,1)} %copy-done.6, bf16[1,1024,1,128]{3,1,2,0:T(8,128)(2,1)S(1)} %all_gather.16), kind=kOutput, calls=%fused_computation.24 | convolution fusion | flops 537395200 | bytes 4980736 | tf_op jit(solution)/shard_map/cgqk,kcd->qcgd/dot_general | solution.py:73
  144.4 1.1 copy.23
  145.5 124.9 %reduce-scatter.3.cloned.1.call-done = f32[128,8]{0,1:T(8,128)} async-done(((f32[4096,8]{0,1:T(8,128)}), f32[128,8]{0,1:T(8,128)}) %reduce-scatter.3.cloned.1.call-update) | async-done | bytes 4112 | tf_op jit(solution)/shard_map/reduce_scatter | solution.py:62
  270.4 1.3 multiply_divide_fusion
  271.7 30.1 %reduce-scatter.5.cloned.1.call-done = f32[256,1,256]{0,2,1:T(8,128)} async-done(((f32[1024,1,256]{0,2,1:T(8,128)}), f32[256,1,256]{0,2,1:T(8,128)}) %reduce-scatter.5.cloned.1.call-update) | async-done | bytes 262160 | tf_op jit(solution)/shard_map/reduce_scatter | solution.py:84
  301.8 1.0 convert.5
  (33 shorter events, 4.7 us)
Async XLA Ops:
  7.2 107.9 %copy-start = (bf16[1,256,4096]{2,1,0:T(8,128)(2,1)S(1)}, bf16[1,256,4096]{2,1,0:T(8,128)(2,1)}, u32[]{:S(2)}) copy-start(bf16[1,256,4096]{2,1,0:T(8,128)(2,1)} %param.15) | copy-start | bytes 6291460
  7.2 107.9 %all-gather.2.cloned.1.call-start = ((), (), s32[]{:S(2)}) async-start(), calls=%async_computation.2 | async-start | bytes 8650752 | tf_op jit(solution)/shard_map/all_gather | solution.py:54
  10.8 259.6 %reduce-scatter.3.cloned.1.call-start = ((), (), s32[]{:S(2)}) async-start(), calls=%async_computation.3 | async-start | bytes 135168 | tf_op jit(solution)/shard_map/reduce_scatter | solution.py:62
  57.4 3.2 %copy-start.1 = (f32[1024,256,8]{1,0,2:T(8,128)}, f32[1024,256,8]{1,0,2:T(8,128)S(1)}, u32[]{:S(2)}) copy-start(f32[1024,256,8]{1,0,2:T(8,128)S(1)} %get-tuple-element.11) | copy-start | bytes 25165828
  115.1 5.9 %copy-start.2 = (f32[1024,256,8]{1,0,2:T(8,128)S(1)}, f32[1024,256,8]{1,0,2:T(8,128)}, u32[]{:S(2)}) copy-start(f32[1024,256,8]{1,0,2:T(8,128)} %copy-done.1) | copy-start | bytes 25165828
  115.1 8.7 %slice-start = ((s8[8388608]{0:T(1024)(128)(4,1)}), s8[4194304]{0:T(1024)(128)(4,1)S(1)}, s32[]{:S(2)}) async-start(s8[8388608]{0:T(1024)(128)(4,1)} %bitcast.152), calls=%async_computation.5 | async-start | bytes 8388608
  121.0 2.8 copy-start.4
  121.0 2.7 slice-start.1
  126.8 174.9 %reduce-scatter.5.cloned.1.call-start = ((), (), s32[]{:S(2)}) async-start(), calls=%async_computation.4 | async-start | bytes 1310720 | tf_op jit(solution)/shard_map/reduce_scatter | solution.py:84
  127.1 5.3 %copy-start.5 = (bf16[1024,256]{1,0:T(8,128)(2,1)S(1)}, bf16[1024,256]{1,0:T(8,128)(2,1)}, u32[]{:S(2)}) copy-start(bf16[1024,256]{1,0:T(8,128)(2,1)} %copy-done.4) | copy-start | bytes 1572868
  137.9 1.9 copy-start.6
  137.9 132.5 %copy-start.3 = (bf16[128,8]{0,1:T(8,128)(2,1)S(1)}, bf16[128,8]{0,1:T(8,128)(2,1)}, u32[]{:S(2)}) copy-start(bf16[128,8]{0,1:T(8,128)(2,1)} %param.14) | copy-start | bytes 6148
Sparse Core Ops, SparseCore 0:
  10.9 104.1 all-gather.1
  127.0 143.3 reduce-scatter.2
  273.1 28.5 reduce-scatter.4

commit v2 on v1

v2 whole, which is shorter than its diff:
```python
import jax
import jax.numpy as jnp
from jax import lax
from jax.experimental import pallas as pl
from jax.experimental.pallas import tpu as pltpu
from jax.sharding import PartitionSpec as P

MESH = pl.DeviceIdType.MESH
HEADS = 8
HEAD = 128
TOK = 256
DOUT = 4096
BLOCKS = 3
AHEAD = 2
SCALE = HEAD**-0.5
LOG2E = 1.4426950408889634
STEP_SCALE = 8192**-0.5
NT = (((1,), (1,)), ((), ()))


def mm(a, b):
    return jnp.dot(a, b, preferred_element_type=jnp.float32)


def kernel(
    q_hbm, k_ref, v_ref, seg_ref, codes_hbm, zero_ref, step_ref, cot_hbm,
    gs_ref, dq_ref, dk_ref, dv_ref,
    q_in, q_f32, codes, cot, cot_t, wbuf, kv, kv_t, seg, bias, qh, xbuf, ebuf, att, rinv, pacc, dkv,
    p1, r1, p2, r2, r3, dsend, drecv,
    in_sem, zs, zr, zf, ys, yr, fs, fr, ps, pr, kvs, kvr, sgs, sgr, s1, t1, s2, t2, s3, t3, gs_s, gs_r,
):
    dp = lax.axis_index("dp")
    s = lax.axis_index("seq")
    core = lax.rem(dp, 2)
    y = dp // 2
    partner = dp + 1 - 2 * core
    yp = lax.rem(y + 1, 4) * 2 + core
    ym = lax.rem(y + 3, 4) * 2 + core
    y2 = lax.rem(y + 2, 4) * 2 + core

    in_codes = pltpu.make_async_copy(codes_hbm, codes, in_sem.at[0])
    in_q = pltpu.make_async_copy(q_hbm, q_in, in_sem.at[1])
    in_cot = pltpu.make_async_copy(cot_hbm, cot, in_sem.at[2])
    in_codes.start()
    in_q.start()
    in_cot.start()

    barrier = pltpu.get_barrier_semaphore()
    for other in (partner, yp, ym, y2):
        pl.semaphore_signal(barrier, inc=1, device_id={"dp": other}, device_id_type=MESH)
    for k in (1, 2, 3):
        pl.semaphore_signal(
            barrier, inc=1, device_id={"seq": lax.rem(s + k, 4)}, device_id_type=MESH
        )

    def rows(block):
        return pl.ds(pl.multiple_of(block * 128, 128), 128)

    def remote(src, dst, send, recv, **to):
        return pltpu.make_async_remote_copy(
            src, dst, send, recv, device_id=to, device_id_type=MESH
        )

    def zcopy(c, block, to, send):
        part = wbuf.at[c, dp, :, rows(block)]
        return remote(part, part, send, zr.at[c, block], seq=to)

    def ycopy(c, k):
        part = wbuf.at[c, dp]
        return remote(part, part, ys.at[c, k], yr.at[c, k], dp=(yp, ym)[k])

    def fcopy(c, k):
        part = wbuf.at[c, (ym, yp)[k], pl.ds(k * 64, 64)]
        return remote(part, part, fs.at[c, k], fr.at[c, k], dp=(yp, ym)[k])

    def pcopy(c, k):
        part = wbuf.at[c, (dp, ym, yp, y2)[k]]
        return remote(part, part, ps.at[c, k], pr.at[c, k], dp=partner)

    def near(to):
        return (jnp.abs(s - to) == 1) | (jnp.abs(s - to) == 2)

    def z_start(c):
        for to in range(4):
            @pl.when(near(to))
            def _():
                zcopy(c, s, to, zs.at[c, to]).start()

    def z_arrive(c):
        @pl.when(s == 2)
        def _():
            zcopy(c, 0, 0, zf.at[c]).wait_recv()
            zcopy(c, 0, 3, zf.at[c]).start()

        @pl.when(s == 1)
        def _():
            zcopy(c, 3, 3, zf.at[c]).wait_recv()
            zcopy(c, 3, 0, zf.at[c]).start()

        for block in range(4):
            known = s == block
            if block == 0:
                known = known | (s == 2)
            if block == 3:
                known = known | (s == 1)

            @pl.when(jnp.logical_not(known))
            def _():
                zcopy(c, block, block, zf.at[c]).wait_recv()

    def make_weight(h):
        part = jnp.transpose(codes[:, h * HEAD : (h + 1) * HEAD].astype(jnp.float32))
        zero = zero_ref[h : h + 1, :].astype(jnp.float32)
        step = step_ref[...].astype(jnp.float32)[h : h + 1, :]
        wbuf[h, dp, :, rows(s)] = ((part - zero) * step).astype(jnp.bfloat16)

    def kv_copy(k):
        return remote(kv.at[2], kv.at[1 - k], kvs.at[k], kvr.at[k], seq=s + 1 + k)

    def seg_copy(k):
        return remote(seg.at[2], seg.at[1 - k], sgs.at[k], sgr.at[k], seq=s + 1 + k)

    in_codes.wait()
    make_weight(0)
    make_weight(1)
    pl.semaphore_wait(barrier, 7)
    z_start(0)
    z_start(1)
    kv[2, 0] = k_ref[...]
    kv[2, 1] = v_ref[...]
    seg[2] = jnp.broadcast_to(seg_ref[...], (8, TOK))
    for k in range(2):
        @pl.when(s + 1 + k < 4)
        def _():
            seg_copy(k).start()
            kv_copy(k).start()

        @pl.when(s - 1 - k < 0)
        def _():
            kv[1 - k] = jnp.zeros((2, TOK, HEAD), jnp.bfloat16)
            seg[1 - k] = jnp.full((8, TOK), -1, jnp.int32)

    for h in range(2, HEADS):
        make_weight(h)
    in_q.wait()
    q_f32[...] = q_in[...].astype(jnp.float32).reshape(TOK * HEADS, HEAD)
    for h in range(HEADS):
        qh[h] = q_f32[pl.ds(h, TOK, stride=HEADS), :].astype(jnp.bfloat16)
    in_cot.wait()

    def turn(i, _):
        part = cot[:, pl.ds(pl.multiple_of(i * 512, 512), 512)].astype(jnp.float32)
        cot_t[pl.ds(pl.multiple_of(i * 512, 512), 512), :] = jnp.transpose(part).astype(
            jnp.bfloat16
        )
        return 0

    lax.fori_loop(0, 8, turn, 0)
    dkv[...] = jnp.zeros((2, BLOCKS * TOK, HEAD), jnp.float32)

    def attention_inputs():
        for k in range(2):
            @pl.when(s - 1 - k >= 0)
            def _():
                remote(
                    kv.at[2], kv.at[1 - k], kvs.at[k], kvr.at[k], seq=s - 1 - k
                ).wait_recv()
                remote(
                    seg.at[2], seg.at[1 - k], sgs.at[k], sgr.at[k], seq=s - 1 - k
                ).wait_recv()

        own = seg_ref[...].astype(jnp.float32)
        for j in range(BLOCKS):
            kv_t[0, :, j * TOK : (j + 1) * TOK] = jnp.transpose(
                kv[j, 0].astype(jnp.float32)
            ).astype(jnp.bfloat16)
            kv_t[1, :, j * TOK : (j + 1) * TOK] = jnp.transpose(
                kv[j, 1].astype(jnp.float32)
            ).astype(jnp.bfloat16)
            for half in range(2):
                row = seg[j, 0:1, half * 128 : (half + 1) * 128].astype(jnp.float32)
                column = jnp.transpose(jnp.broadcast_to(row, (128, 128)))
                column = jnp.concatenate([column, column], axis=1)
                allowed = column == own
                if j == BLOCKS - 1:
                    key_pos = half * 128 + lax.broadcasted_iota(jnp.int32, (128, TOK), 0)
                    query_pos = lax.broadcasted_iota(jnp.int32, (128, TOK), 1)
                    allowed = allowed & (key_pos <= query_pos)
                bias[j * TOK + half * 128 : j * TOK + (half + 1) * 128, :] = jnp.where(
                    allowed, jnp.float32(0.0), jnp.float32(-1e30)
                )

    def forward(h):
        q = qh[h]
        top = jnp.full((1, TOK), -1e30, jnp.float32)
        for j in range(BLOCKS):
            x = lax.dot_general(kv[j, 0], q, NT, preferred_element_type=jnp.float32)
            x = x * (SCALE * LOG2E) + bias[j * TOK : (j + 1) * TOK, :]
            xbuf[j * TOK : (j + 1) * TOK, :] = x
            top = jnp.maximum(top, jnp.max(x, axis=0, keepdims=True))
        total = jnp.zeros((1, TOK), jnp.float32)
        out = jnp.zeros((HEAD, TOK), jnp.float32)
        for j in range(BLOCKS):
            e = jnp.exp2(xbuf[j * TOK : (j + 1) * TOK, :] - top)
            total = total + jnp.sum(e, axis=0, keepdims=True)
            low = e.astype(jnp.bfloat16)
            ebuf[h, j * TOK : (j + 1) * TOK, :] = low
            out = out + mm(kv_t[1, :, j * TOK : (j + 1) * TOK], low)
        inv = 1.0 / total
        rinv[h] = jnp.broadcast_to(inv, (8, TOK))
        att[h] = (out * inv).astype(jnp.bfloat16)

    def backward(h):
        att_h = att[h]
        go = jnp.zeros((HEAD, TOK), jnp.float32)
        for d in range(8):
            w = wbuf[h, d]
            go = go + mm(w, cot_t[d * 512 : (d + 1) * 512, :])
            gw = mm(att_h, cot[:, d * 512 : (d + 1) * 512])
            pacc[d % 2, d // 2, pl.ds(h, 1), :] = jnp.sum(
                gw * w.astype(jnp.float32), axis=0, keepdims=True
            )
        go = go * rinv[h, 0:1, :]
        delta = jnp.sum(go * att_h.astype(jnp.float32), axis=0, keepdims=True)
        go_low = go.astype(jnp.bfloat16)
        go_t = jnp.transpose(go).astype(jnp.bfloat16)
        q = qh[h]
        dq = jnp.zeros((HEAD, TOK), jnp.float32)
        for j in range(BLOCKS):
            part = slice(j * TOK, (j + 1) * TOK)
            e = ebuf[h, part, :]
            dprob = mm(kv[j, 1], go_low)
            ds = (e.astype(jnp.float32) * (dprob - delta)).astype(jnp.bfloat16)
            dq = dq + mm(kv_t[0, :, part], ds)
            dkv[0, part, :] += mm(ds, q)
            dkv[1, part, :] += mm(e, go_t)
        dq_ref[h] = jnp.transpose(dq * SCALE).astype(jnp.bfloat16)

    def step(i, _):
        @pl.when(i < HEADS)
        def _():
            @pl.when(i + 2 < HEADS)
            def _():
                z_start(i + 2)

            z_arrive(i)
            ycopy(i, 0).start()
            ycopy(i, 1).start()
            pcopy(i, 0).start()

            @pl.when(i == 0)
            def _():
                attention_inputs()

            forward(i)

        @pl.when((i >= AHEAD) & (i < HEADS + AHEAD))
        def _():
            c = i - AHEAD
            ycopy(c, 0).wait_recv()
            fcopy(c, 0).start()
            pcopy(c, 1).start()
            ycopy(c, 1).wait_recv()
            fcopy(c, 1).start()
            pcopy(c, 2).start()

        @pl.when(i >= AHEAD + 1)
        def _():
            c = i - AHEAD - 1
            fcopy(c, 0).wait_recv()
            fcopy(c, 1).wait_recv()
            pcopy(c, 3).start()
            for k in range(4):
                pcopy(c, k).wait_recv()
            backward(c)

        return 0

    lax.fori_loop(0, HEADS + AHEAD + 1, step, 0)

    def d_copy(k, to):
        return remote(dsend.at[k], drecv.at[k], gs_s.at[k], gs_r.at[k], seq=to)

    for k in range(2):
        part = slice((1 - k) * TOK, (2 - k) * TOK)
        dsend[k, 0] = dkv[0, part, :].astype(jnp.bfloat16)
        dsend[k, 1] = dkv[1, part, :].astype(jnp.bfloat16)

        @pl.when(s - 1 - k >= 0)
        def _():
            d_copy(k, s - 1 - k).start()

        @pl.when(s + 1 + k >= 4)
        def _():
            drecv[k] = jnp.zeros((2, TOK, HEAD), jnp.bfloat16)

    first = remote(pacc.at[1 - core], r1, s1, t1, dp=partner)
    first.start()
    first.wait_recv()
    p1[...] = pacc[core] + r1[...]

    def second(k):
        to = lax.rem(s + 1 + k, 4)
        return remote(p1.at[:, :, rows(to)], r2.at[k], s2.at[k], t2.at[k], seq=to)

    for k in range(3):
        second(k).start()
    mine = p1[:, :, rows(s)]
    for k in range(3):
        second(k).wait_recv()
        mine = mine + r2[k]
    p2[...] = mine

    def third(k):
        to = lax.rem(y + 1 + k, 4)
        return remote(p2.at[to], r3.at[k], s3.at[k], t3.at[k], dp=to * 2 + core)

    for k in range(3):
        third(k).start()
    total = p2[y]
    for k in range(3):
        third(k).wait_recv()
        total = total + r3[k]
    gs_ref[...] = total * STEP_SCALE / step_ref[...].astype(jnp.float32)

    for k in range(2):
        @pl.when(s + 1 + k < 4)
        def _():
            d_copy(k, s + 1 + k).wait_recv()

    own = slice(2 * TOK, 3 * TOK)
    recv = drecv[...].astype(jnp.float32)
    dk_ref[...] = ((dkv[0, own, :] + recv[0, 0] + recv[1, 0]) * SCALE).astype(jnp.bfloat16)
    dv_ref[...] = (dkv[1, own, :] + recv[0, 1] + recv[1, 1]).astype(jnp.bfloat16)

    def sent(c, _):
        for to in range(4):
            @pl.when(near(to))
            def _():
                zcopy(c, s, to, zs.at[c, to]).wait_send()

        @pl.when(s == 2)
        def _():
            zcopy(c, 0, 3, zf.at[c]).wait_send()

        @pl.when(s == 1)
        def _():
            zcopy(c, 3, 0, zf.at[c]).wait_send()

        for k in range(2):
            ycopy(c, k).wait_send()
            fcopy(c, k).wait_send()
        for k in range(4):
            pcopy(c, k).wait_send()
        return 0

    lax.fori_loop(0, HEADS, sent, 0)
    for k in range(2):
        @pl.when(s + 1 + k < 4)
        def _():
            seg_copy(k).wait_send()
            kv_copy(k).wait_send()

        @pl.when(s - 1 - k >= 0)
        def _():
            d_copy(k, s - 1 - k).wait_send()

    first.wait_send()
    for k in range(3):
        second(k).wait_send()
        third(k).wait_send()


def local(queries, keys, values, segment_ids, codes, zero_points, step_sizes, cotangent):
    bf16, f32, i32 = jnp.bfloat16, jnp.float32, jnp.int32
    dma = pltpu.SemaphoreType.DMA
    vmem = pltpu.VMEM
    in_vmem = pl.BlockSpec(memory_space=pltpu.VMEM)
    anywhere = pl.BlockSpec(memory_space=pl.ANY)
    steps, dq, dk, dv = pl.pallas_call(
        kernel,
        out_shape=(
            jax.ShapeDtypeStruct((HEADS, 128), f32),
            jax.ShapeDtypeStruct((HEADS, TOK, HEAD), bf16),
            jax.ShapeDtypeStruct((TOK, HEAD), bf16),
            jax.ShapeDtypeStruct((TOK, HEAD), bf16),
        ),
        in_specs=[anywhere, in_vmem, in_vmem, in_vmem, anywhere, in_vmem, in_vmem, anywhere],
        out_specs=(in_vmem, in_vmem, in_vmem, in_vmem),
        scratch_shapes=[
            vmem((TOK, HEADS, HEAD), bf16),
            vmem((TOK * HEADS, HEAD), f32),
            vmem((128, HEADS * HEAD), i32),
            vmem((TOK, DOUT), bf16),
            vmem((DOUT, TOK), bf16),
            vmem((HEADS, 8, HEAD, 512), bf16),
            vmem((BLOCKS, 2, TOK, HEAD), bf16),
            vmem((2, HEAD, BLOCKS * TOK), bf16),
            vmem((BLOCKS, 8, TOK), i32),
            vmem((BLOCKS * TOK, TOK), f32),
            vmem((HEADS, TOK, HEAD), bf16),
            vmem((BLOCKS * TOK, TOK), f32),
            vmem((HEADS, BLOCKS * TOK, TOK), bf16),
            vmem((HEADS, HEAD, TOK), bf16),
            vmem((HEADS, 8, TOK), f32),
            vmem((2, 4, HEADS, 512), f32),
            vmem((2, BLOCKS * TOK, HEAD), f32),
            vmem((4, HEADS, 512), f32),
            vmem((4, HEADS, 512), f32),
            vmem((4, HEADS, 128), f32),
            vmem((3, 4, HEADS, 128), f32),
            vmem((3, HEADS, 128), f32),
            vmem((2, 2, TOK, HEAD), bf16),
            vmem((2, 2, TOK, HEAD), bf16),
            dma((3,)),
            dma((HEADS, 4)), dma((HEADS, 4)), dma((HEADS,)),
            dma((HEADS, 2)), dma((HEADS, 2)), dma((HEADS, 2)), dma((HEADS, 2)),
            dma((HEADS, 4)), dma((HEADS, 4)),
            dma((2,)), dma((2,)), dma((2,)), dma((2,)),
            dma, dma, dma((3,)), dma((3,)), dma((3,)), dma((3,)),
            dma((2,)), dma((2,)),
        ],
        compiler_params=pltpu.CompilerParams(
            collective_id=0, has_side_effects=True, vmem_limit_bytes=56 * 2**20
        ),
        name="fused",
    )(
        queries[0], keys.reshape(TOK, HEAD), values.reshape(TOK, HEAD), segment_ids,
        codes, zero_points.T, step_sizes.T, cotangent[0],
    )
    grad_queries = jnp.transpose(dq, (1, 0, 2))[None]
    return (steps.T, grad_queries, dk.reshape(1, TOK, 1, HEAD), dv.reshape(1, TOK, 1, HEAD))


def solution(mesh):
    in_specs = (
        P("dp", "seq", "tensor", None),
        P("dp", "seq", "tensor", None),
        P("dp", "seq", "tensor", None),
        P("dp", "seq"),
        P(("dp", "seq"), "tensor"),
        P(("dp", "seq"), "tensor"),
        P(("dp", "seq"), "tensor"),
        P("dp", "seq", None),
    )
    out_specs = (
        P(("dp", "seq"), "tensor"),
        P("dp", "seq", "tensor", None),
        P("dp", "seq", "tensor", None),
        P("dp", "seq", "tensor", None),
    )
    return jax.shard_map(local, mesh=mesh, in_specs=in_specs, out_specs=out_specs, check_vma=False)
```

time: 312 us -> 91.4 us (0.29)
  waiting for transfers between devices: 207 us -> 0 us
  Pallas kernels: 0 us -> 83.7 us
  blocking collectives: 41.2 us -> 0 us
  matrix products: 28.7 us -> 0 us
  between operations: 14 us -> 0.64 us
  other arithmetic: 9.14 us -> 0 us
  local copies, waits for them, and re-layouts: 9.92 us -> 6.4 us
    reduce_scatter x2 -> x0, waiting for transfers between devices: 155 us -> none  [the longest x1 125 us: local(): lax.psum_scatter(partial_steps, ('dp', 'seq'), scatter_dimension=0, tiled...]
    pallas_call x0 -> x1, Pallas kernels: none -> 83.7 us  [local(): pl.pallas_call(kernel, out_shape=(jax.ShapeDtypeStruct((HEADS, 128), f32)...]
    all_gather x1 -> x0, waiting for transfers between devices: 52.5 us -> none  [local(): weight_all = lax.all_gather(weight_loc, ('dp', 'seq'), axis=0, tiled=True)]
    all_gather x3 -> x0, blocking collectives: 41.2 us -> none  [the longest x1 14.7 us: local(): lax.all_gather(values, 'seq', axis=1, tiled=True)]
    dot_general x8 -> x0, matrix products: 28.7 us -> none  [the longest x1 5.9 us: local(): grad_acc = jnp.dot(columns, weight_all, preferred_element_type=jnp.float32)]
    convert_element_type x4 -> x0, other arithmetic: 3.53 us -> none  [the longest x1 1.46 us: local(): weight_loc = (centered.astype(jnp.float32) * jnp.repeat(step_sizes.astype...]
    unnamed x23 -> x4, local copies, waits for them, and re-layouts: 8.59 us -> 6.4 us
  transfers between devices with their start and end apart: 3 -> 0, of which waited for: 3 -> 0; matrix products, arithmetic and copies ran while one was open for 9% -> 0% of each run, Pallas kernels for 0% -> 0%
where the time goes in v2:
time: 91.4 us; the launch traced here: 90.7 us
  Pallas kernels  83.7 us (92%)
  local copies, waits for them, and re-layouts  6.4 us (7%)
    pallas_call x1, Pallas kernels, local(): pl.pallas_call(kernel, out_shape=(jax.ShapeDtypeStruct((HEADS, 128), f32)...  83.7 us
    unnamed x4, local copies, waits for them, and re-layouts  6.4 us

profile of v2, /device:TPU:2, one launch (start us, length us, event | category | flops | bytes accessed | tf_op | source)
XLA Modules:
  0.0 90.7 jit_solution(2215563647688494787)
XLA Ops:
  0.6 83.7 %fused.1 = (f32[8,128]{1,0:T(8,128)}, bf16[8,256,128]{2,1,0:T(8,128)(2,1)}, bf16[256,128]{1,0:T(8,128)(2,1)}, bf16[256,128]{1,0:T(8,128)(2,1)}) custom-call(bf16[256,8,128]{2,1,0:T(8,128)(2,1)} %bitcast.14, bf16[256,128]{1,0:T(8,128)(2,1)} %bitcast.15, bf16[256,128]{1,0:T(8,128)(2,1)} %bitcast.16, s32[1,256]{1,0:T(1,128)} %seg_ref.1, s32[128,1024]{1,0:T(8,128)} %codes_hbm.1, ...), custom_call_target="tpu_custom_call" | custom-call | tf_op jit(solution)/shard_map/fused/pallas_call | solution.py:380
  84.3 2.2 %copy.12 = bf16[1,256,8,128]{3,2,1,0:T(8,128)(2,1)} copy(bf16[1,256,8,128]{3,1,2,0:T(8,128)(2,1)} %bitcast.13) | data formatting | bytes 1048576
  86.5 1.3 %copy.16 = f32[128,8]{0,1:T(8,128)} copy(f32[128,8]{0,1:T(8,128)} %bitcast.20) | data formatting | bytes 8192
  87.8 1.5 %copy.17 = bf16[1,256,1,128]{3,1,2,0:T(8,128)(2,1)} copy(bf16[1,256,1,128]{3,1,2,0:T(8,128)(2,1)} %bitcast.18) | data formatting | bytes 131072
  89.3 1.5 %copy.18 = bf16[1,256,1,128]{3,1,2,0:T(8,128)(2,1)} copy(bf16[1,256,1,128]{3,1,2,0:T(8,128)(2,1)} %bitcast.17) | data formatting | bytes 131072

commit v3 on v2

v3 whole, which is shorter than its diff:
```python
import jax
import jax.numpy as jnp
from jax import lax
from jax.experimental import pallas as pl
from jax.experimental.pallas import tpu as pltpu
from jax.sharding import PartitionSpec as P

MESH = pl.DeviceIdType.MESH
HEADS = 8
HEAD = 128
TOK = 256
DOUT = 4096
BLOCKS = 3
WAYS = 7
SCALE = HEAD**-0.5
LOG2E = 1.4426950408889634
STEP_SCALE = 8192**-0.5
NT = (((1,), (1,)), ((), ()))


def mm(a, b):
    return jnp.dot(a, b, preferred_element_type=jnp.float32)


def kernel(
    q_hbm, k_ref, v_ref, seg_ref, codes_hbm, zero_ref, step_ref, cot_hbm,
    gs_ref, dq_ref, dk_ref, dv_ref,
    q_in, q_f32, codes, cot, cot_t, wbuf, kv, kv_t, seg, bias, qh, xbuf, ebuf, att, rinv, pacc, dkv,
    p1, r1, p2, r2, r3, dsend, drecv,
    in_sem, zs, zr, os, ors, ys, yr, fs, fr, ps, pr, kvs, kvr, sgs, sgr, s1, t1, s2, t2, s3, t3, gs_s, gs_r,
):
    dp = lax.axis_index("dp")
    s = lax.axis_index("seq")
    core = lax.rem(dp, 2)
    y = dp // 2
    partner = dp + 1 - 2 * core
    yp = lax.rem(y + 1, 4)
    ym = lax.rem(y + 3, 4)
    y2 = lax.rem(y + 2, 4)

    in_codes = pltpu.make_async_copy(codes_hbm, codes, in_sem.at[0])
    in_q = pltpu.make_async_copy(q_hbm, q_in, in_sem.at[1])
    in_cot = pltpu.make_async_copy(cot_hbm, cot, in_sem.at[2])
    in_codes.start()
    in_q.start()

    def cot_piece(d, slot):
        source = pl.multiple_of(d * 512 + lax.rem(slot + s, 4) * 128, 128)
        target = pl.multiple_of(d * 512 + slot * 128, 128)
        return pltpu.make_async_copy(
            cot_hbm.at[:, pl.ds(source, 128)], cot.at[:, pl.ds(target, 128)], in_sem.at[2]
        )

    def cot_start(d, _):
        for slot in range(4):
            cot_piece(d, slot).start()
        return 0


    barrier = pltpu.get_barrier_semaphore()
    for other in (partner, yp * 2 + core, ym * 2 + core, y2 * 2 + core):
        pl.semaphore_signal(barrier, inc=1, device_id={"dp": other}, device_id_type=MESH)
    for k in (1, 2, 3):
        pl.semaphore_signal(
            barrier, inc=1, device_id={"seq": lax.rem(s + k, 4)}, device_id_type=MESH
        )

    def remote(src, dst, send, recv, **to):
        return pltpu.make_async_remote_copy(
            src, dst, send, recv, device_id=to, device_id_type=MESH
        )

    def zcopy(c, slot, to, to_slot, send):
        return remote(
            wbuf.at[c, core, y, slot], wbuf.at[c, core, y, to_slot], send, zr.at[c, to_slot], seq=to
        )

    def bcopy(slot, to, to_slot, send):
        c = WAYS
        return remote(
            wbuf.at[c, core, :, slot], wbuf.at[c, core, :, to_slot], send, zr.at[c, to_slot], seq=to
        )

    def ycopy(c, k):
        part = wbuf.at[c, core, y, pl.ds(1, 3)]
        return remote(part, part, ys.at[c, k], yr.at[c, k], dp=(yp, ym)[k] * 2 + core)

    def ocopy(c, k):
        part = wbuf.at[c, core, y, 0]
        return remote(part, part, os.at[c, k], ors.at[c, k], dp=(yp, ym)[k] * 2 + core)

    def fcopy(c, k):
        part = wbuf.at[c, core, (ym, yp)[k], pl.ds(k * 2, 2)]
        return remote(part, part, fs.at[c, k], fr.at[c, k], dp=(yp, ym)[k] * 2 + core)

    def hcopy(k):
        part = wbuf.at[WAYS, core, (ym, yp)[k], 0, pl.ds(k * 64, 64)]
        return remote(part, part, fs.at[WAYS, k], fr.at[WAYS, k], dp=(yp, ym)[k] * 2 + core)

    def pcopy(c, k):
        part = wbuf.at[c, core, (y, ym, yp, y2)[k]]
        return remote(part, part, ps.at[c, k], pr.at[c, k], dp=partner)

    def wcopy():
        part = wbuf.at[WAYS, core]
        return remote(part, part, ps.at[WAYS, 0], pr.at[WAYS, 0], dp=partner)

    def near(to):
        return (jnp.abs(s - to) == 1) | (jnp.abs(s - to) == 2)

    inner = (s == 1) | (s == 2)
    end = jnp.where(s == 2, 3, 0)
    end_slot = jnp.where(s == 2, 1, 3)

    def own_start(c):
        for k in range(2):
            ocopy(c, k).start()

    def z_start(copy):
        for to in range(4):
            @pl.when(near(to))
            def _():
                copy(0, to, lax.rem(s + 4 - to, 4), to).start()

    def z_arrive(copy):
        @pl.when(inner)
        def _():
            copy(0, s, 2, 0).wait_recv()
            copy(2, end, end_slot, 4).start()

        for slot in range(1, 4):
            def wait():
                copy(0, s, slot, 0).wait_recv()

            if slot == 2:
                pl.when(jnp.logical_not(inner))(wait)
            else:
                wait()

    def way_a(c):
        return lambda slot, to, to_slot, k: zcopy(c, slot, to, to_slot, zs.at[c, k])

    def way_b(slot, to, to_slot, k):
        return bcopy(slot, to, to_slot, zs.at[WAYS, k])

    def make_weight(h):
        part = jnp.transpose(codes[:, h * HEAD : (h + 1) * HEAD].astype(jnp.float32))
        zero = zero_ref[h : h + 1, :].astype(jnp.float32)
        step = step_ref[...].astype(jnp.float32)[h : h + 1, :]
        wbuf[h, core, y, 0] = ((part - zero) * step).astype(jnp.bfloat16)

    def kv_copy(k):
        return remote(kv.at[2], kv.at[1 - k], kvs.at[k], kvr.at[k], seq=s + 1 + k)

    def seg_copy(k):
        return remote(seg.at[2], seg.at[1 - k], sgs.at[k], sgr.at[k], seq=s + 1 + k)

    in_codes.wait()
    make_weight(0)
    pl.semaphore_wait(barrier, 7)
    z_start(way_a(0))
    own_start(0)
    make_weight(1)
    z_start(way_a(1))
    own_start(1)
    for h in (WAYS, *range(2, WAYS)):
        make_weight(h)
        own_start(h)
    lax.fori_loop(0, 8, cot_start, 0)

    def kv_start():
        kv[2, 0] = k_ref[...]
        kv[2, 1] = v_ref[...]
        seg[2] = jnp.broadcast_to(seg_ref[...], (8, TOK))
        for k in range(2):
            @pl.when(s + 1 + k < 4)
            def _():
                seg_copy(k).start()
                kv_copy(k).start()

            @pl.when(s - 1 - k < 0)
            def _():
                kv[1 - k] = jnp.zeros((2, TOK, HEAD), jnp.bfloat16)
                seg[1 - k] = jnp.full((8, TOK), -1, jnp.int32)

    def query_inputs():
        in_q.wait()
        q_f32[...] = q_in[...].astype(jnp.float32).reshape(TOK * HEADS, HEAD)
        for h in range(HEADS):
            qh[h] = q_f32[pl.ds(h, TOK, stride=HEADS), :].astype(jnp.bfloat16)
        dkv[...] = jnp.zeros((2, BLOCKS * TOK, HEAD), jnp.float32)

    def cot_inputs():
        in_cot.wait()

        def turn(i, _):
            part = cot[:, pl.ds(pl.multiple_of(i * 512, 512), 512)].astype(jnp.float32)
            cot_t[pl.ds(pl.multiple_of(i * 512, 512), 512), :] = jnp.transpose(part).astype(
                jnp.bfloat16
            )
            return 0

        lax.fori_loop(0, 8, turn, 0)

    def attention_inputs():
        for k in range(2):
            @pl.when(s - 1 - k >= 0)
            def _():
                remote(
                    kv.at[2], kv.at[1 - k], kvs.at[k], kvr.at[k], seq=s - 1 - k
                ).wait_recv()
                remote(
                    seg.at[2], seg.at[1 - k], sgs.at[k], sgr.at[k], seq=s - 1 - k
                ).wait_recv()

        own = seg_ref[...].astype(jnp.float32)
        for j in range(BLOCKS):
            kv_t[0, :, j * TOK : (j + 1) * TOK] = jnp.transpose(
                kv[j, 0].astype(jnp.float32)
            ).astype(jnp.bfloat16)
            kv_t[1, :, j * TOK : (j + 1) * TOK] = jnp.transpose(
                kv[j, 1].astype(jnp.float32)
            ).astype(jnp.bfloat16)
            for half in range(2):
                row = seg[j, 0:1, half * 128 : (half + 1) * 128].astype(jnp.float32)
                column = jnp.transpose(jnp.broadcast_to(row, (128, 128)))
                column = jnp.concatenate([column, column], axis=1)
                allowed = column == own
                if j == BLOCKS - 1:
                    key_pos = half * 128 + lax.broadcasted_iota(jnp.int32, (128, TOK), 0)
                    query_pos = lax.broadcasted_iota(jnp.int32, (128, TOK), 1)
                    allowed = allowed & (key_pos <= query_pos)
                bias[j * TOK + half * 128 : j * TOK + (half + 1) * 128, :] = jnp.where(
                    allowed, jnp.float32(0.0), jnp.float32(-1e30)
                )

    def forward(h):
        q = qh[h]
        top = jnp.full((1, TOK), -1e30, jnp.float32)
        for j in range(BLOCKS):
            x = lax.dot_general(kv[j, 0], q, NT, preferred_element_type=jnp.float32)
            x = x * (SCALE * LOG2E) + bias[j * TOK : (j + 1) * TOK, :]
            xbuf[j * TOK : (j + 1) * TOK, :] = x
            top = jnp.maximum(top, jnp.max(x, axis=0, keepdims=True))
        total = jnp.zeros((1, TOK), jnp.float32)
        out = jnp.zeros((HEAD, TOK), jnp.float32)
        for j in range(BLOCKS):
            e = jnp.exp2(xbuf[j * TOK : (j + 1) * TOK, :] - top)
            total = total + jnp.sum(e, axis=0, keepdims=True)
            low = e.astype(jnp.bfloat16)
            ebuf[h, j * TOK : (j + 1) * TOK, :] = low
            out = out + mm(kv_t[1, :, j * TOK : (j + 1) * TOK], low)
        inv = 1.0 / total
        rinv[h] = jnp.broadcast_to(inv, (8, TOK))
        att[h] = (out * inv).astype(jnp.bfloat16)

    def d_copy(k, to):
        return remote(dsend.at[k], drecv.at[k], gs_s.at[k], gs_r.at[k], seq=to)

    def d_start(k):
        part = slice((1 - k) * TOK, (2 - k) * TOK)
        dsend[k, 0] = dkv[0, part, :].astype(jnp.bfloat16)
        dsend[k, 1] = dkv[1, part, :].astype(jnp.bfloat16)

        @pl.when(s - 1 - k >= 0)
        def _():
            d_copy(k, s - 1 - k).start()

        @pl.when(s + 1 + k >= 4)
        def _():
            drecv[k] = jnp.zeros((2, TOK, HEAD), jnp.bfloat16)

    first = remote(pacc.at[1 - core], r1, s1, t1, dp=partner)

    def second(k):
        to = lax.rem(s + 1 + k, 4)
        return remote(p1.at[:, :, pl.ds((1 + k) * 128, 128)], r2.at[k], s2.at[k], t2.at[k], seq=to)

    def third(k):
        to = lax.rem(y + 1 + k, 4)
        return remote(p2.at[to], r3.at[k], s3.at[k], t3.at[k], dp=to * 2 + core)

    def after_first():
        first.wait_recv()
        p1[...] = pacc[core] + r1[...]
        for k in range(3):
            second(k).start()

    def after_second():
        mine = p1[:, :, 0:128]
        for k in range(3):
            second(k).wait_recv()
            mine = mine + r2[k]
        p2[...] = mine
        for k in range(3):
            third(k).start()

    def weight_block(h, d):
        return jnp.concatenate([wbuf[h, d % 2, d // 2, b] for b in range(4)], axis=1)

    def backward(h):
        last = h == WAYS - 1
        att_h = att[h]
        for d in range(8):
            gw = mm(att_h, cot[:, d * 512 : (d + 1) * 512])
            pacc[d % 2, d // 2, pl.ds(h, 1), :] = jnp.sum(
                gw * weight_block(h, d).astype(jnp.float32), axis=0, keepdims=True
            )

        @pl.when(last)
        def _():
            first.start()

        go = jnp.zeros((HEAD, TOK), jnp.float32)
        for d in range(8):
            go = go + mm(weight_block(h, d), cot_t[d * 512 : (d + 1) * 512, :])
        go = go * rinv[h, 0:1, :]
        delta = jnp.sum(go * att_h.astype(jnp.float32), axis=0, keepdims=True)
        go_low = go.astype(jnp.bfloat16)
        go_t = jnp.transpose(go).astype(jnp.bfloat16)
        q = qh[h]
        dq = jnp.zeros((HEAD, TOK), jnp.float32)
        for j in range(BLOCKS):
            part = slice(j * TOK, (j + 1) * TOK)
            e = ebuf[h, part, :]
            dprob = mm(kv[j, 1], go_low)
            ds = (e.astype(jnp.float32) * (dprob - delta)).astype(jnp.bfloat16)
            dq = dq + mm(kv_t[0, :, part], ds)
            dkv[0, part, :] += mm(ds, q)
            dkv[1, part, :] += mm(e, go_t)
            if j < 2:
                @pl.when(last)
                def _():
                    d_start(1 - j)
                    if j == 0:
                        after_first()
        q_f32[pl.ds(h, TOK, stride=HEADS), :] = jnp.transpose(dq * SCALE)

    def step(i, _):
        @pl.when(i < WAYS)
        def _():
            @pl.when(i + 2 < WAYS)
            def _():
                z_start(way_a(i + 2))

            @pl.when(i + 2 == WAYS)
            def _():
                for k in range(2):
                    hcopy(k).wait_recv()
                z_start(way_b)

            z_arrive(way_a(i))
            ycopy(i, 0).start()
            ycopy(i, 1).start()
            pcopy(i, 0).start()

            @pl.when(i == 0)
            def _():
                kv_start()
                query_inputs()

            @pl.when(i == 1)
            def _():
                for k in range(2):
                    ocopy(WAYS, k).wait_recv()
                    hcopy(k).start()
                cot_inputs()

        @pl.when(i == 2)
        def _():
            attention_inputs()

        @pl.when((i >= 2) & (i < HEADS + 2))
        def _():
            forward(i - 2)

        @pl.when((i >= 1) & (i < WAYS + 1))
        def _():
            c = i - 1
            for k in range(2):
                ocopy(c, k).wait_recv()
                ycopy(c, k).wait_recv()
                fcopy(c, k).start()
                pcopy(c, 1 + k).start()

        @pl.when((i >= 2) & (i < WAYS + 2))
        def _():
            c = i - 2
            fcopy(c, 0).wait_recv()
            fcopy(c, 1).wait_recv()
            pcopy(c, 3).start()

        @pl.when(i == WAYS)
        def _():
            z_arrive(way_b)
            wcopy().start()

        @pl.when((i >= 3) & (i != WAYS + 2))
        def _():
            c = jnp.where(i > WAYS + 2, WAYS - 1, i - 3)
            for k in range(4):
                pcopy(c, k).wait_recv()

        @pl.when(i == WAYS + 2)
        def _():
            wcopy().wait_recv()

        @pl.when(i >= 3)
        def _():
            backward(jnp.where(i > WAYS + 2, WAYS - 1, jnp.where(i == WAYS + 2, WAYS, i - 3)))

        return 0

    lax.fori_loop(0, HEADS + 3, step, 0)

    after_second()
    dq_ref[...] = q_f32[...].reshape(TOK, HEADS, HEAD).astype(jnp.bfloat16)
    total = p2[y]
    for k in range(3):
        third(k).wait_recv()
        total = total + r3[k]
    gs_ref[...] = total * STEP_SCALE / step_ref[...].astype(jnp.float32)

    for k in range(2):
        @pl.when(s + 1 + k < 4)
        def _():
            d_copy(k, s + 1 + k).wait_recv()

    own = slice(2 * TOK, 3 * TOK)
    recv = drecv[...].astype(jnp.float32)
    dk_ref[...] = ((dkv[0, own, :] + recv[0, 0] + recv[1, 0]) * SCALE).astype(jnp.bfloat16)
    dv_ref[...] = (dkv[1, own, :] + recv[0, 1] + recv[1, 1]).astype(jnp.bfloat16)

    def z_sent(copy):
        for to in range(4):
            @pl.when(near(to))
            def _():
                copy(0, to, lax.rem(s + 4 - to, 4), to).wait_send()

        @pl.when(inner)
        def _():
            copy(2, end, end_slot, 4).wait_send()

    def sent(c, _):
        z_sent(way_a(c))
        for k in range(2):
            ocopy(c, k).wait_send()
            ycopy(c, k).wait_send()
            fcopy(c, k).wait_send()
        for k in range(4):
            pcopy(c, k).wait_send()
        return 0

    lax.fori_loop(0, WAYS, sent, 0)
    z_sent(way_b)
    for k in range(2):
        ocopy(WAYS, k).wait_send()
        hcopy(k).wait_send()
    wcopy().wait_send()
    for k in range(2):
        @pl.when(s + 1 + k < 4)
        def _():
            seg_copy(k).wait_send()
            kv_copy(k).wait_send()

        @pl.when(s - 1 - k >= 0)
        def _():
            d_copy(k, s - 1 - k).wait_send()

    first.wait_send()
    for k in range(3):
        second(k).wait_send()
        third(k).wait_send()


def hand_over(*refs):
    for k in range(4):
        refs[4 + k][...] = refs[k][...]


def local(queries, keys, values, segment_ids, codes, zero_points, step_sizes, cotangent):
    bf16, f32, i32 = jnp.bfloat16, jnp.float32, jnp.int32
    dma = pltpu.SemaphoreType.DMA
    vmem = pltpu.VMEM
    in_vmem = pl.BlockSpec(memory_space=pltpu.VMEM)
    anywhere = pl.BlockSpec(memory_space=pl.ANY)
    results = pl.pallas_call(
        kernel,
        out_shape=(
            jax.ShapeDtypeStruct((HEADS, 128), f32),
            jax.ShapeDtypeStruct((TOK, HEADS, HEAD), bf16),
            jax.ShapeDtypeStruct((TOK, HEAD), bf16),
            jax.ShapeDtypeStruct((TOK, HEAD), bf16),
        ),
        in_specs=[anywhere, in_vmem, in_vmem, in_vmem, anywhere, in_vmem, in_vmem, anywhere],
        out_specs=(in_vmem, in_vmem, in_vmem, in_vmem),
        scratch_shapes=[
            vmem((TOK, HEADS, HEAD), bf16),
            vmem((TOK * HEADS, HEAD), f32),
            vmem((128, HEADS * HEAD), i32),
            vmem((TOK, DOUT), bf16),
            vmem((DOUT, TOK), bf16),
            vmem((HEADS, 2, 4, 4, HEAD, 128), bf16),
            vmem((BLOCKS, 2, TOK, HEAD), bf16),
            vmem((2, HEAD, BLOCKS * TOK), bf16),
            vmem((BLOCKS, 8, TOK), i32),
            vmem((BLOCKS * TOK, TOK), f32),
            vmem((HEADS, TOK, HEAD), bf16),
            vmem((BLOCKS * TOK, TOK), f32),
            vmem((HEADS, BLOCKS * TOK, TOK), bf16),
            vmem((HEADS, HEAD, TOK), bf16),
            vmem((HEADS, 8, TOK), f32),
            vmem((2, 4, HEADS, 512), f32),
            vmem((2, BLOCKS * TOK, HEAD), f32),
            vmem((4, HEADS, 512), f32),
            vmem((4, HEADS, 512), f32),
            vmem((4, HEADS, 128), f32),
            vmem((3, 4, HEADS, 128), f32),
            vmem((3, HEADS, 128), f32),
            vmem((2, 2, TOK, HEAD), bf16),
            vmem((2, 2, TOK, HEAD), bf16),
            dma((3,)),
            dma((HEADS, 5)), dma((HEADS, 4)),
            dma((HEADS, 2)), dma((HEADS, 2)), dma((HEADS, 2)), dma((HEADS, 2)), dma((HEADS, 2)), dma((HEADS, 2)),
            dma((HEADS, 4)), dma((HEADS, 4)),
            dma((2,)), dma((2,)), dma((2,)), dma((2,)),
            dma, dma, dma((3,)), dma((3,)), dma((3,)), dma((3,)),
            dma((2,)), dma((2,)),
        ],
        compiler_params=pltpu.CompilerParams(
            collective_id=0, has_side_effects=True, vmem_limit_bytes=56 * 2**20
        ),
        name="fused",
    )(
        queries[0], keys.reshape(TOK, HEAD), values.reshape(TOK, HEAD), segment_ids,
        codes, zero_points.T, step_sizes.T, cotangent[0],
    )
    steps, dq, dk, dv = pl.pallas_call(
        hand_over,
        out_shape=[jax.ShapeDtypeStruct(r.shape, r.dtype) for r in results],
        in_specs=[in_vmem] * 4,
        out_specs=[in_vmem] * 4,
        name="hand_over",
    )(*results)
    return (steps.T, dq[None], dk.reshape(1, TOK, 1, HEAD), dv.reshape(1, TOK, 1, HEAD))


def solution(mesh):
    in_specs = (
        P("dp", "seq", "tensor", None),
        P("dp", "seq", "tensor", None),
        P("dp", "seq", "tensor", None),
        P("dp", "seq"),
        P(("dp", "seq"), "tensor"),
        P(("dp", "seq"), "tensor"),
        P(("dp", "seq"), "tensor"),
        P("dp", "seq", None),
    )
    out_specs = (
        P(("dp", "seq"), "tensor"),
        P("dp", "seq", "tensor", None),
        P("dp", "seq", "tensor", None),
        P("dp", "seq", "tensor", None),
    )
    return jax.shard_map(local, mesh=mesh, in_specs=in_specs, out_specs=out_specs, check_vma=False)
```

time: 91.4 us -> 76.6 us (0.84)
  Pallas kernels: 83.7 us -> 75.8 us
  local copies, waits for them, and re-layouts: 6.4 us -> 0 us
    pallas_call x1, Pallas kernels: 83.7 us -> 73.9 us  [local(): pl.pallas_call(kernel, out_shape=(jax.ShapeDtypeStruct((HEADS, 128), f32)...]
    unnamed x4 -> x0, local copies, waits for them, and re-layouts: 6.4 us -> none
    pallas_call x0 -> x1, Pallas kernels: none -> 1.91 us  [local(): pl.pallas_call(hand_over, out_shape=[jax.ShapeDtypeStruct(r.shape, r.dtyp...]
where the time goes in v3:
time: 76.6 us; the launch traced here: 76.4 us
  Pallas kernels  75.8 us (99%)
    pallas_call x1, Pallas kernels, local(): pl.pallas_call(kernel, out_shape=(jax.ShapeDtypeStruct((HEADS, 128), f32)...  73.9 us
    pallas_call x1, Pallas kernels, local(): pl.pallas_call(hand_over, out_shape=[jax.ShapeDtypeStruct(r.shape, r.dtyp...  1.91 us

profile of v3, /device:TPU:2, one launch (start us, length us, event | category | flops | bytes accessed | tf_op | source)
XLA Modules:
  0.0 76.4 jit_solution(15692166160598356169)
XLA Ops:
  0.6 73.9 %fused.1 = (f32[8,128]{1,0:T(8,128)}, bf16[256,8,128]{2,1,0:T(8,128)(2,1)}, bf16[256,128]{1,0:T(8,128)(2,1)}, bf16[256,128]{1,0:T(8,128)(2,1)}) custom-call(bf16[256,8,128]{2,1,0:T(8,128)(2,1)} %bitcast.11, bf16[256,128]{1,0:T(8,128)(2,1)} %bitcast.12, bf16[256,128]{1,0:T(8,128)(2,1)} %bitcast.13, s32[1,256]{1,0:T(1,128)} %seg_ref.1, s32[128,1024]{1,0:T(8,128)} %codes_hbm.1, ...), custom_call_target="tpu_custom_call" | custom-call | tf_op jit(solution)/shard_map/fused/pallas_call | solution.py:487
  74.5 1.9 %hand_over.1 = (f32[8,128]{1,0:T(8,128)}, bf16[256,8,128]{2,1,0:T(8,128)(2,1)}, bf16[256,128]{1,0:T(8,128)(2,1)}, bf16[256,128]{1,0:T(8,128)(2,1)}) custom-call(f32[8,128]{1,0:T(8,128)} %get-tuple-element.12.refs_0_, bf16[256,8,128]{2,1,0:T(8,128)(2,1)} %get-tuple-element.13.refs_1_, bf16[256,128]{1,0:T(8,128)(2,1)} %get-tuple-element.14.refs_2_, ...), custom_call_target="tpu_custom_call" | custom-call | tf_op jit(solution)/shard_map/hand_over/pallas_call | solution.py:538

commit v4 on v3

--- a/solution.py
+++ b/solution.py
@@ -25,9 +25,9 @@
 def kernel(
     q_hbm, k_ref, v_ref, seg_ref, codes_hbm, zero_ref, step_ref, cot_hbm,
     gs_ref, dq_ref, dk_ref, dv_ref,
-    q_in, q_f32, codes, cot, cot_t, wbuf, kv, kv_t, seg, bias, qh, xbuf, ebuf, att, rinv, pacc, dkv,
-    p1, r1, p2, r2, r3, dsend, drecv,
-    in_sem, zs, zr, os, ors, ys, yr, fs, fr, ps, pr, kvs, kvr, sgs, sgr, s1, t1, s2, t2, s3, t3, gs_s, gs_r,
+    q_in, q_f32, codes, cot, cot_t, wbuf, kv, kv_t, seg, bias, qh, xbuf, ebuf, att, rinv, gout, pacc, dkv,
+    p1, r1, p2, r2, r3, dfar, dnear, rfar, rnear,
+    in_sem, zs, zr, os, ors, ys, yr, fs, fr, ps, pr, kvs, kvr, sgs, sgr, s1, t1, s2, t2, s3, t3, ds_s, ds_r,
 ):
     dp = lax.axis_index("dp")
     s = lax.axis_index("seq")
@@ -254,86 +254,102 @@
         rinv[h] = jnp.broadcast_to(inv, (8, TOK))
         att[h] = (out * inv).astype(jnp.bfloat16)
 
-    def d_copy(k, to):
-        return remote(dsend.at[k], drecv.at[k], gs_s.at[k], gs_r.at[k], seq=to)
-
-    def d_start(k):
-        part = slice((1 - k) * TOK, (2 - k) * TOK)
-        dsend[k, 0] = dkv[0, part, :].astype(jnp.bfloat16)
-        dsend[k, 1] = dkv[1, part, :].astype(jnp.bfloat16)
-
-        @pl.when(s - 1 - k >= 0)
-        def _():
-            d_copy(k, s - 1 - k).start()
-
-        @pl.when(s + 1 + k >= 4)
-        def _():
-            drecv[k] = jnp.zeros((2, TOK, HEAD), jnp.bfloat16)
-
-    first = remote(pacc.at[1 - core], r1, s1, t1, dp=partner)
-
-    def second(k):
-        to = lax.rem(s + 1 + k, 4)
-        return remote(p1.at[:, :, pl.ds((1 + k) * 128, 128)], r2.at[k], s2.at[k], t2.at[k], seq=to)
+    def far_copy(kind, to):
+        return remote(dfar.at[kind], rfar.at[kind], ds_s.at[0, kind], ds_r.at[0, kind], seq=to)
+
+    def near_copy(kind, to):
+        return remote(dnear.at[kind], rnear.at[kind], ds_s.at[1, kind], ds_r.at[1, kind], seq=to)
+
+    def far_start(kind):
+        dfar[kind] = dkv[kind, 0:TOK, :].astype(jnp.bfloat16)
+
+        @pl.when(s >= 2)
+        def _():
+            far_copy(kind, s - 1).start()
+
+        @pl.when((s == 0) | (s == 3))
+        def _():
+            rfar[kind] = jnp.zeros((TOK, HEAD), jnp.bfloat16)
+
+    def near_start(kind):
+        @pl.when(inner)
+        def _():
+            far_copy(kind, s + 1).wait_recv()
+
+        both = dkv[kind, TOK : 2 * TOK, :] + rfar[kind].astype(jnp.float32)
+        dnear[kind] = both.astype(jnp.bfloat16)
+
+        @pl.when(s >= 1)
+        def _():
+            near_copy(kind, s - 1).start()
+
+        @pl.when(s == 3)
+        def _():
+            rnear[kind] = jnp.zeros((TOK, HEAD), jnp.bfloat16)
+
+    def first(k):
+        part = pacc.at[:, :, :, pl.ds((1 + k) * 128, 128)]
+        return remote(part, r1.at[k], s1.at[k], t1.at[k], seq=lax.rem(s + 1 + k, 4))
+
+    second = remote(p1.at[1 - core], r2, s2, t2, dp=partner)
 
     def third(k):
         to = lax.rem(y + 1 + k, 4)
         return remote(p2.at[to], r3.at[k], s3.at[k], t3.at[k], dp=to * 2 + core)
 
     def after_first():
-        first.wait_recv()
-        p1[...] = pacc[core] + r1[...]
+        mine = pacc[:, :, :, 0:128]
         for k in range(3):
-            second(k).start()
+            first(k).wait_recv()
+            mine = mine + r1[k]
+        p1[...] = mine
+        second.start()
 
     def after_second():
-        mine = p1[:, :, 0:128]
-        for k in range(3):
-            second(k).wait_recv()
-            mine = mine + r2[k]
-        p2[...] = mine
+        second.wait_recv()
+        p2[...] = p1[core] + r2[...]
         for k in range(3):
             third(k).start()
 
     def weight_block(h, d):
         return jnp.concatenate([wbuf[h, d % 2, d // 2, b] for b in range(4)], axis=1)
 
-    def backward(h):
-        last = h == WAYS - 1
-        att_h = att[h]
+    def kv_all(k):
+        return jnp.concatenate([kv[j, k] for j in range(BLOCKS)], axis=0)
+
+    def group_sums(heads):
+        att_h = jnp.concatenate([att[h] for h in heads], axis=0)
         for d in range(8):
             gw = mm(att_h, cot[:, d * 512 : (d + 1) * 512])
-            pacc[d % 2, d // 2, pl.ds(h, 1), :] = jnp.sum(
-                gw * weight_block(h, d).astype(jnp.float32), axis=0, keepdims=True
-            )
-
-        @pl.when(last)
-        def _():
-            first.start()
-
-        go = jnp.zeros((HEAD, TOK), jnp.float32)
+            for n, h in enumerate(heads):
+                w = weight_block(h, d).astype(jnp.float32)
+                pacc[d % 2, d // 2, pl.ds(h, 1), :] = jnp.sum(
+                    gw[n * HEAD : (n + 1) * HEAD] * w, axis=0, keepdims=True
+                )
+
+    def grad_out(heads):
+        go = jnp.zeros((len(heads) * HEAD, TOK), jnp.float32)
         for d in range(8):
-            go = go + mm(weight_block(h, d), cot_t[d * 512 : (d + 1) * 512, :])
-        go = go * rinv[h, 0:1, :]
-        delta = jnp.sum(go * att_h.astype(jnp.float32), axis=0, keepdims=True)
-        go_low = go.astype(jnp.bfloat16)
-        go_t = jnp.transpose(go).astype(jnp.bfloat16)
-        q = qh[h]
-        dq = jnp.zeros((HEAD, TOK), jnp.float32)
-        for j in range(BLOCKS):
-            part = slice(j * TOK, (j + 1) * TOK)
-            e = ebuf[h, part, :]
-            dprob = mm(kv[j, 1], go_low)
-            ds = (e.astype(jnp.float32) * (dprob - delta)).astype(jnp.bfloat16)
-            dq = dq + mm(kv_t[0, :, part], ds)
-            dkv[0, part, :] += mm(ds, q)
-            dkv[1, part, :] += mm(e, go_t)
-            if j < 2:
-                @pl.when(last)
-                def _():
-                    d_start(1 - j)
-                    if j == 0:
-                        after_first()
+            w = jnp.concatenate([weight_block(h, d) for h in heads], axis=0)
+            go = go + mm(w, cot_t[d * 512 : (d + 1) * 512, :])
+        for n, h in enumerate(heads):
+            gout[h] = go[n * HEAD : (n + 1) * HEAD] * rinv[h, 0:1, :]
+
+    def attention(h, last=False):
+        go = gout[h]
+        delta = jnp.sum(go * att[h].astype(jnp.float32), axis=0, keepdims=True)
+        e = ebuf[h]
+        dkv[1] += mm(e, jnp.transpose(go).astype(jnp.bfloat16))
+        if last:
+            far_start(1)
+        dprob = mm(kv_all(1), go.astype(jnp.bfloat16))
+        ds = (e.astype(jnp.float32) * (dprob - delta)).astype(jnp.bfloat16)
+        dkv[0] += mm(ds, qh[h])
+        if last:
+            far_start(0)
+            after_first()
+            near_start(1)
+        dq = mm(kv_t[0], ds)
         q_f32[pl.ds(h, TOK, stride=HEADS), :] = jnp.transpose(dq * SCALE)
 
     def step(i, _):
@@ -370,9 +386,13 @@
         def _():
             attention_inputs()
 
-        @pl.when((i >= 2) & (i < HEADS + 2))
-        def _():
-            forward(i - 2)
+        def forward_turn(h, _):
+            forward(h)
+            return 0
+
+        first_forward = jnp.where(i < 4, 2 * i - 4, i)
+        forwards = jnp.where((i < 2) | (i >= HEADS), 0, jnp.where(i < 4, 2, 1))
+        lax.fori_loop(first_forward, first_forward + forwards, forward_turn, 0)
 
         @pl.when((i >= 1) & (i < WAYS + 1))
         def _():
@@ -395,24 +415,46 @@
             z_arrive(way_b)
             wcopy().start()
 
-        @pl.when((i >= 3) & (i != WAYS + 2))
-        def _():
-            c = jnp.where(i > WAYS + 2, WAYS - 1, i - 3)
+        @pl.when((i >= 3) & (i < WAYS + 2))
+        def _():
             for k in range(4):
-                pcopy(c, k).wait_recv()
-
-        @pl.when(i == WAYS + 2)
+                pcopy(i - 3, k).wait_recv()
+
+        @pl.when(i == WAYS + 1)
         def _():
             wcopy().wait_recv()
 
-        @pl.when(i >= 3)
-        def _():
-            backward(jnp.where(i > WAYS + 2, WAYS - 1, jnp.where(i == WAYS + 2, WAYS, i - 3)))
-
+        @pl.when((i == 4) | (i == 6) | (i == 8))
+        def _():
+            heads = (jnp.where(i == 8, 5, i - 4), jnp.where(i == 8, 7, i - 3))
+            group_sums(heads)
+            grad_out(heads)
+
+        def attention_turn(h, _):
+            @pl.when(h == 4)
+            def _():
+                group_sums((h,))
+                grad_out((h,))
+
+            attention(h)
+            return 0
+
+        first_head = jnp.where(i == 9, 7, jnp.where(i == 8, 5, i - 4))
+        count = jnp.where(i < 4, 0, jnp.where(i == 7, 2, 1))
+        lax.fori_loop(first_head, first_head + count, attention_turn, 0)
         return 0
 
-    lax.fori_loop(0, HEADS + 3, step, 0)
-
+    lax.fori_loop(0, HEADS + 2, step, 0)
+
+    final = WAYS - 1
+    for k in range(4):
+        pcopy(final, k).wait_recv()
+    group_sums((final,))
+    for k in range(3):
+        first(k).start()
+    grad_out((final,))
+    attention(final, last=True)
+    near_start(0)
     after_second()
     dq_ref[...] = q_f32[...].reshape(TOK, HEADS, HEAD).astype(jnp.bfloat16)
     total = p2[y]
@@ -420,16 +462,6 @@
         third(k).wait_recv()
         total = total + r3[k]
     gs_ref[...] = total * STEP_SCALE / step_ref[...].astype(jnp.float32)
-
-    for k in range(2):
-        @pl.when(s + 1 + k < 4)
-        def _():
-            d_copy(k, s + 1 + k).wait_recv()
-
-    own = slice(2 * TOK, 3 * TOK)
-    recv = drecv[...].astype(jnp.float32)
-    dk_ref[...] = ((dkv[0, own, :] + recv[0, 0] + recv[1, 0]) * SCALE).astype(jnp.bfloat16)
-    dv_ref[...] = (dkv[1, own, :] + recv[0, 1] + recv[1, 1]).astype(jnp.bfloat16)
 
     def z_sent(copy):
         for to in range(4):
@@ -463,14 +495,27 @@
             seg_copy(k).wait_send()
             kv_copy(k).wait_send()
 
-        @pl.when(s - 1 - k >= 0)
-        def _():
-            d_copy(k, s - 1 - k).wait_send()
-
-    first.wait_send()
     for k in range(3):
-        second(k).wait_send()
+        first(k).wait_send()
         third(k).wait_send()
+    second.wait_send()
+
+    own = slice(2 * TOK, 3 * TOK)
+    for kind, scale, out_ref in ((1, 1.0, dv_ref), (0, SCALE, dk_ref)):
+        @pl.when(s < 3)
+        def _():
+            near_copy(kind, s + 1).wait_recv()
+
+        total = dkv[kind, own, :] + rnear[kind].astype(jnp.float32)
+        out_ref[...] = (total * scale).astype(jnp.bfloat16)
+
+        @pl.when(s >= 2)
+        def _():
+            far_copy(kind, s - 1).wait_send()
+
+        @pl.when(s >= 1)
+        def _():
+            near_copy(kind, s - 1).wait_send()
 
 
 def hand_over(*refs):
@@ -510,22 +555,25 @@
             vmem((HEADS, BLOCKS * TOK, TOK), bf16),
             vmem((HEADS, HEAD, TOK), bf16),
             vmem((HEADS, 8, TOK), f32),
+            vmem((HEADS, HEAD, TOK), f32),
             vmem((2, 4, HEADS, 512), f32),
             vmem((2, BLOCKS * TOK, HEAD), f32),
-            vmem((4, HEADS, 512), f32),
-            vmem((4, HEADS, 512), f32),
+            vmem((2, 4, HEADS, 128), f32),
+            vmem((3, 2, 4, HEADS, 128), f32),
             vmem((4, HEADS, 128), f32),
-            vmem((3, 4, HEADS, 128), f32),
+            vmem((4, HEADS, 128), f32),
             vmem((3, HEADS, 128), f32),
-            vmem((2, 2, TOK, HEAD), bf16),
-            vmem((2, 2, TOK, HEAD), bf16),
+            vmem((2, TOK, HEAD), bf16),
+            vmem((2, TOK, HEAD), bf16),
+            vmem((2, TOK, HEAD), bf16),
+            vmem((2, TOK, HEAD), bf16),
             dma((3,)),
             dma((HEADS, 5)), dma((HEADS, 4)),
             dma((HEADS, 2)), dma((HEADS, 2)), dma((HEADS, 2)), dma((HEADS, 2)), dma((HEADS, 2)), dma((HEADS, 2)),
             dma((HEADS, 4)), dma((HEADS, 4)),
             dma((2,)), dma((2,)), dma((2,)), dma((2,)),
-            dma, dma, dma((3,)), dma((3,)), dma((3,)), dma((3,)),
-            dma((2,)), dma((2,)),
+            dma((3,)), dma((3,)), dma, dma, dma((3,)), dma((3,)),
+            dma((2, 2)), dma((2, 2)),
         ],
         compiler_params=pltpu.CompilerParams(
             collective_id=0, has_side_effects=True, vmem_limit_bytes=56 * 2**20

time: 76.6 us -> 70.8 us (0.924)
  Pallas kernels: 75.8 us -> 69.5 us
    pallas_call x1, Pallas kernels: 73.9 us -> 67.6 us  [local(): pl.pallas_call(kernel, out_shape=(jax.ShapeDtypeStruct((HEADS, 128), f32)...]
where the time goes in v4:
time: 70.8 us; the launch traced here: 70.2 us
  Pallas kernels  69.5 us (98%)
    pallas_call x1, Pallas kernels, local(): pl.pallas_call(kernel, out_shape=(jax.ShapeDtypeStruct((HEADS, 128), f32)...  67.6 us
    pallas_call x1, Pallas kernels, local(): pl.pallas_call(hand_over, out_shape=[jax.ShapeDtypeStruct(r.shape, r.dtyp...  1.91 us

profile of v4, /device:TPU:2, one launch (start us, length us, event | category | flops | bytes accessed | tf_op | source)
XLA Modules:
  0.0 70.2 jit_solution(15881162539520044789)
XLA Ops:
  0.6 67.6 %fused.1 = (f32[8,128]{1,0:T(8,128)}, bf16[256,8,128]{2,1,0:T(8,128)(2,1)}, bf16[256,128]{1,0:T(8,128)(2,1)}, bf16[256,128]{1,0:T(8,128)(2,1)}) custom-call(bf16[256,8,128]{2,1,0:T(8,128)(2,1)} %bitcast.11, bf16[256,128]{1,0:T(8,128)(2,1)} %bitcast.12, bf16[256,128]{1,0:T(8,128)(2,1)} %bitcast.13, s32[1,256]{1,0:T(1,128)} %seg_ref.1, s32[128,1024]{1,0:T(8,128)} %codes_hbm.1, ...), custom_call_target="tpu_custom_call" | custom-call | tf_op jit(solution)/shard_map/fused/pallas_call | solution.py:532
  68.3 1.9 %hand_over.1 = (f32[8,128]{1,0:T(8,128)}, bf16[256,8,128]{2,1,0:T(8,128)(2,1)}, bf16[256,128]{1,0:T(8,128)(2,1)}, bf16[256,128]{1,0:T(8,128)(2,1)}) custom-call(f32[8,128]{1,0:T(8,128)} %get-tuple-element.12.refs_0_, bf16[256,8,128]{2,1,0:T(8,128)(2,1)} %get-tuple-element.13.refs_1_, bf16[256,128]{1,0:T(8,128)(2,1)} %get-tuple-element.14.refs_2_, ...), custom_call_target="tpu_custom_call" | custom-call | tf_op jit(solution)/shard_map/hand_over/pallas_call | solution.py:586

commit v5 on v4

--- a/solution.py
+++ b/solution.py
@@ -122,12 +122,13 @@
             def _():
                 copy(0, to, lax.rem(s + 4 - to, 4), to).start()
 
-    def z_arrive(copy):
+    def z_pass(copy):
         @pl.when(inner)
         def _():
             copy(0, s, 2, 0).wait_recv()
             copy(2, end, end_slot, 4).start()
 
+    def z_arrive(copy):
         for slot in range(1, 4):
             def wait():
                 copy(0, s, slot, 0).wait_recv()
@@ -150,10 +151,22 @@
         wbuf[h, core, y, 0] = ((part - zero) * step).astype(jnp.bfloat16)
 
     def kv_copy(k):
-        return remote(kv.at[2], kv.at[1 - k], kvs.at[k], kvr.at[k], seq=s + 1 + k)
+        return remote(kv.at[2 - k], kv.at[1 - k], kvs.at[k], kvr.at[k], seq=s + 1)
 
     def seg_copy(k):
-        return remote(seg.at[2], seg.at[1 - k], sgs.at[k], sgr.at[k], seq=s + 1 + k)
+        return remote(seg.at[2 - k], seg.at[1 - k], sgs.at[k], sgr.at[k], seq=s + 1)
+
+    def kv_send(k):
+        @pl.when((s < 3) & (s >= k))
+        def _():
+            seg_copy(k).start()
+            kv_copy(k).start()
+
+    def kv_arrive(k):
+        @pl.when(s >= 1 + k)
+        def _():
+            remote(kv.at[2 - k], kv.at[1 - k], kvs.at[k], kvr.at[k], seq=s - 1).wait_recv()
+            remote(seg.at[2 - k], seg.at[1 - k], sgs.at[k], sgr.at[k], seq=s - 1).wait_recv()
 
     in_codes.wait()
     make_weight(0)
@@ -163,25 +176,27 @@
     make_weight(1)
     z_start(way_a(1))
     own_start(1)
-    for h in (WAYS, *range(2, WAYS)):
+    make_weight(2)
+    z_start(way_a(2))
+    own_start(2)
+    for h in (WAYS, *range(3, WAYS)):
         make_weight(h)
         own_start(h)
     lax.fori_loop(0, 8, cot_start, 0)
+    z_pass(way_a(0))
+    z_pass(way_a(1))
 
     def kv_start():
         kv[2, 0] = k_ref[...]
         kv[2, 1] = v_ref[...]
         seg[2] = jnp.broadcast_to(seg_ref[...], (8, TOK))
         for k in range(2):
-            @pl.when(s + 1 + k < 4)
-            def _():
-                seg_copy(k).start()
-                kv_copy(k).start()
-
             @pl.when(s - 1 - k < 0)
             def _():
                 kv[1 - k] = jnp.zeros((2, TOK, HEAD), jnp.bfloat16)
                 seg[1 - k] = jnp.full((8, TOK), -1, jnp.int32)
+
+        kv_send(0)
 
     def query_inputs():
         in_q.wait()
@@ -203,16 +218,7 @@
         lax.fori_loop(0, 8, turn, 0)
 
     def attention_inputs():
-        for k in range(2):
-            @pl.when(s - 1 - k >= 0)
-            def _():
-                remote(
-                    kv.at[2], kv.at[1 - k], kvs.at[k], kvr.at[k], seq=s - 1 - k
-                ).wait_recv()
-                remote(
-                    seg.at[2], seg.at[1 - k], sgs.at[k], sgr.at[k], seq=s - 1 - k
-                ).wait_recv()
-
+        kv_arrive(1)
         own = seg_ref[...].astype(jnp.float32)
         for j in range(BLOCKS):
             kv_t[0, :, j * TOK : (j + 1) * TOK] = jnp.transpose(
@@ -352,23 +358,38 @@
         dq = mm(kv_t[0], ds)
         q_f32[pl.ds(h, TOK, stride=HEADS), :] = jnp.transpose(dq * SCALE)
 
+    def y_start(c):
+        z_arrive(way_a(c))
+        ycopy(c, 0).start()
+        ycopy(c, 1).start()
+        pcopy(c, 0).start()
+
+    y_start(0)
+
     def step(i, _):
         @pl.when(i < WAYS)
         def _():
-            @pl.when(i + 2 < WAYS)
-            def _():
-                z_start(way_a(i + 2))
-
-            @pl.when(i + 2 == WAYS)
+            @pl.when(i + 3 < WAYS)
+            def _():
+                z_start(way_a(i + 3))
+
+            @pl.when(i + 4 == WAYS)
             def _():
                 for k in range(2):
                     hcopy(k).wait_recv()
                 z_start(way_b)
 
-            z_arrive(way_a(i))
-            ycopy(i, 0).start()
-            ycopy(i, 1).start()
-            pcopy(i, 0).start()
+            @pl.when(i + 2 < WAYS)
+            def _():
+                z_pass(way_a(i + 2))
+
+            @pl.when(i + 1 == WAYS)
+            def _():
+                z_pass(way_b)
+
+            @pl.when(i + 1 < WAYS)
+            def _():
+                y_start(i + 1)
 
             @pl.when(i == 0)
             def _():
@@ -381,18 +402,6 @@
                     ocopy(WAYS, k).wait_recv()
                     hcopy(k).start()
                 cot_inputs()
-
-        @pl.when(i == 2)
-        def _():
-            attention_inputs()
-
-        def forward_turn(h, _):
-            forward(h)
-            return 0
-
-        first_forward = jnp.where(i < 4, 2 * i - 4, i)
-        forwards = jnp.where((i < 2) | (i >= HEADS), 0, jnp.where(i < 4, 2, 1))
-        lax.fori_loop(first_forward, first_forward + forwards, forward_turn, 0)
 
         @pl.when((i >= 1) & (i < WAYS + 1))
         def _():
@@ -410,41 +419,58 @@
             fcopy(c, 1).wait_recv()
             pcopy(c, 3).start()
 
+        @pl.when(i == 2)
+        def _():
+            kv_arrive(0)
+            kv_send(1)
+
+        @pl.when(i == 3)
+        def _():
+            attention_inputs()
+
         @pl.when(i == WAYS)
         def _():
             z_arrive(way_b)
             wcopy().start()
 
-        @pl.when((i >= 3) & (i < WAYS + 2))
+        def forward_turn(h, _):
+            forward(h)
+            return 0
+
+        first_forward = jnp.where(i == 3, 0, jnp.where(i == 4, 4, 7))
+        forwards = jnp.where(i == 3, 4, jnp.where(i == 4, 3, jnp.where(i == 5, 1, 0)))
+        lax.fori_loop(first_forward, first_forward + forwards, forward_turn, 0)
+
+        def attention_turn(n, _):
+            attention(jnp.where(i == 8, 5 + 2 * n, jnp.where(i == 7, 4, i - 4 + n)))
+            return 0
+
+        count = jnp.where(i < 4, 0, jnp.where((i == 6) | (i == 8), 2, 1))
+        lax.fori_loop(0, count, attention_turn, 0)
+
+        @pl.when((i >= 2) & (i < WAYS + 1))
         def _():
             for k in range(4):
-                pcopy(i - 3, k).wait_recv()
-
-        @pl.when(i == WAYS + 1)
+                pcopy(i - 2, k).wait_recv()
+
+        @pl.when(i == WAYS)
         def _():
             wcopy().wait_recv()
 
-        @pl.when((i == 4) | (i == 6) | (i == 8))
-        def _():
-            heads = (jnp.where(i == 8, 5, i - 4), jnp.where(i == 8, 7, i - 3))
+        @pl.when((i == 3) | (i == 5) | (i == WAYS))
+        def _():
+            heads = (jnp.where(i == WAYS, 5, i - 3), jnp.where(i == WAYS, 7, i - 2))
             group_sums(heads)
             grad_out(heads)
 
-        def attention_turn(h, _):
-            @pl.when(h == 4)
-            def _():
-                group_sums((h,))
-                grad_out((h,))
-
-            attention(h)
-            return 0
-
-        first_head = jnp.where(i == 9, 7, jnp.where(i == 8, 5, i - 4))
-        count = jnp.where(i < 4, 0, jnp.where(i == 7, 2, 1))
-        lax.fori_loop(first_head, first_head + count, attention_turn, 0)
+        @pl.when(i == 6)
+        def _():
+            group_sums((4,))
+            grad_out((4,))
+
         return 0
 
-    lax.fori_loop(0, HEADS + 2, step, 0)
+    lax.fori_loop(0, HEADS + 1, step, 0)
 
     final = WAYS - 1
     for k in range(4):
@@ -490,7 +516,7 @@
         hcopy(k).wait_send()
     wcopy().wait_send()
     for k in range(2):
-        @pl.when(s + 1 + k < 4)
+        @pl.when((s < 3) & (s >= k))
         def _():
             seg_copy(k).wait_send()
             kv_copy(k).wait_send()

time: 70.8 us -> 69 us (0.975)
  Pallas kernels: 69.5 us -> 67.6 us
    pallas_call x1, Pallas kernels: 67.6 us -> 65.6 us  [local(): pl.pallas_call(kernel, out_shape=(jax.ShapeDtypeStruct((HEADS, 128), f32)...]
where the time goes in v5:
time: 69 us; the launch traced here: 68.2 us
  Pallas kernels  67.6 us (98%)
    pallas_call x1, Pallas kernels, local(): pl.pallas_call(kernel, out_shape=(jax.ShapeDtypeStruct((HEADS, 128), f32)...  65.6 us
    pallas_call x1, Pallas kernels, local(): pl.pallas_call(hand_over, out_shape=[jax.ShapeDtypeStruct(r.shape, r.dtyp...  1.91 us

profile of v5, /device:TPU:2, one launch (start us, length us, event | category | flops | bytes accessed | tf_op | source)
XLA Modules:
  0.0 68.2 jit_solution(9517329129086785472)
XLA Ops:
  0.6 65.6 %fused.1 = (f32[8,128]{1,0:T(8,128)}, bf16[256,8,128]{2,1,0:T(8,128)(2,1)}, bf16[256,128]{1,0:T(8,128)(2,1)}, bf16[256,128]{1,0:T(8,128)(2,1)}) custom-call(bf16[256,8,128]{2,1,0:T(8,128)(2,1)} %bitcast.11, bf16[256,128]{1,0:T(8,128)(2,1)} %bitcast.12, bf16[256,128]{1,0:T(8,128)(2,1)} %bitcast.13, s32[1,256]{1,0:T(1,128)} %seg_ref.1, s32[128,1024]{1,0:T(8,128)} %codes_hbm.1, ...), custom_call_target="tpu_custom_call" | custom-call | tf_op jit(solution)/shard_map/fused/pallas_call | solution.py:558
  66.3 1.9 %hand_over.1 = (f32[8,128]{1,0:T(8,128)}, bf16[256,8,128]{2,1,0:T(8,128)(2,1)}, bf16[256,128]{1,0:T(8,128)(2,1)}, bf16[256,128]{1,0:T(8,128)(2,1)}) custom-call(f32[8,128]{1,0:T(8,128)} %get-tuple-element.12.refs_0_, bf16[256,8,128]{2,1,0:T(8,128)(2,1)} %get-tuple-element.13.refs_1_, bf16[256,128]{1,0:T(8,128)(2,1)} %get-tuple-element.14.refs_2_, ...), custom_call_target="tpu_custom_call" | custom-call | tf_op jit(solution)/shard_map/hand_over/pallas_call | solution.py:612

commit v6 on v5

--- a/solution.py
+++ b/solution.py
@@ -294,17 +294,17 @@
             rnear[kind] = jnp.zeros((TOK, HEAD), jnp.bfloat16)
 
     def first(k):
-        part = pacc.at[:, :, :, pl.ds((1 + k) * 128, 128)]
-        return remote(part, r1.at[k], s1.at[k], t1.at[k], seq=lax.rem(s + 1 + k, 4))
+        to = lax.rem(y + 1 + k, 4)
+        return remote(pacc.at[:, to], r1.at[k], s1.at[k], t1.at[k], dp=to * 2 + core)
 
     second = remote(p1.at[1 - core], r2, s2, t2, dp=partner)
 
     def third(k):
-        to = lax.rem(y + 1 + k, 4)
-        return remote(p2.at[to], r3.at[k], s3.at[k], t3.at[k], dp=to * 2 + core)
+        part = p2.at[:, pl.ds((1 + k) * 128, 128)]
+        return remote(part, r3.at[k], s3.at[k], t3.at[k], seq=lax.rem(s + 1 + k, 4))
 
     def after_first():
-        mine = pacc[:, :, :, 0:128]
+        mine = pacc[:, y]
         for k in range(3):
             first(k).wait_recv()
             mine = mine + r1[k]
@@ -354,7 +354,6 @@
         if last:
             far_start(0)
             after_first()
-            near_start(1)
         dq = mm(kv_t[0], ds)
         q_f32[pl.ds(h, TOK, stride=HEADS), :] = jnp.transpose(dq * SCALE)
 
@@ -480,10 +479,11 @@
         first(k).start()
     grad_out((final,))
     attention(final, last=True)
+    near_start(1)
+    after_second()
     near_start(0)
-    after_second()
     dq_ref[...] = q_f32[...].reshape(TOK, HEADS, HEAD).astype(jnp.bfloat16)
-    total = p2[y]
+    total = p2[:, 0:128]
     for k in range(3):
         third(k).wait_recv()
         total = total + r3[k]
@@ -584,10 +584,10 @@
             vmem((HEADS, HEAD, TOK), f32),
             vmem((2, 4, HEADS, 512), f32),
             vmem((2, BLOCKS * TOK, HEAD), f32),
-            vmem((2, 4, HEADS, 128), f32),
-            vmem((3, 2, 4, HEADS, 128), f32),
-            vmem((4, HEADS, 128), f32),
-            vmem((4, HEADS, 128), f32),
+            vmem((2, HEADS, 512), f32),
+            vmem((3, 2, HEADS, 512), f32),
+            vmem((HEADS, 512), f32),
+            vmem((HEADS, 512), f32),
             vmem((3, HEADS, 128), f32),
             vmem((2, TOK, HEAD), bf16),
             vmem((2, TOK, HEAD), bf16),

time: 69 us -> 68.1 us (0.987)
  Pallas kernels: 67.6 us -> 66.4 us
    pallas_call x1, Pallas kernels: 65.6 us -> 64.5 us  [local(): pl.pallas_call(kernel, out_shape=(jax.ShapeDtypeStruct((HEADS, 128), f32)...]
where the time goes in v6:
time: 68.1 us; the launch traced here: 67.1 us
  Pallas kernels  66.4 us (98%)
    pallas_call x1, Pallas kernels, local(): pl.pallas_call(kernel, out_shape=(jax.ShapeDtypeStruct((HEADS, 128), f32)...  64.5 us
    pallas_call x1, Pallas kernels, local(): pl.pallas_call(hand_over, out_shape=[jax.ShapeDtypeStruct(r.shape, r.dtyp...  1.91 us

profile of v6, /device:TPU:2, one launch (start us, length us, event | category | flops | bytes accessed | tf_op | source)
XLA Modules:
  0.0 67.1 jit_solution(4529255255532451937)
XLA Ops:
  0.6 64.5 %fused.1 = (f32[8,128]{1,0:T(8,128)}, bf16[256,8,128]{2,1,0:T(8,128)(2,1)}, bf16[256,128]{1,0:T(8,128)(2,1)}, bf16[256,128]{1,0:T(8,128)(2,1)}) custom-call(bf16[256,8,128]{2,1,0:T(8,128)(2,1)} %bitcast.11, bf16[256,128]{1,0:T(8,128)(2,1)} %bitcast.12, bf16[256,128]{1,0:T(8,128)(2,1)} %bitcast.13, s32[1,256]{1,0:T(1,128)} %seg_ref.1, s32[128,1024]{1,0:T(8,128)} %codes_hbm.1, ...), custom_call_target="tpu_custom_call" | custom-call | tf_op jit(solution)/shard_map/fused/pallas_call | solution.py:558
  65.2 1.9 %hand_over.1 = (f32[8,128]{1,0:T(8,128)}, bf16[256,8,128]{2,1,0:T(8,128)(2,1)}, bf16[256,128]{1,0:T(8,128)(2,1)}, bf16[256,128]{1,0:T(8,128)(2,1)}) custom-call(f32[8,128]{1,0:T(8,128)} %get-tuple-element.12.refs_0_, bf16[256,8,128]{2,1,0:T(8,128)(2,1)} %get-tuple-element.13.refs_1_, bf16[256,128]{1,0:T(8,128)(2,1)} %get-tuple-element.14.refs_2_, ...), custom_call_target="tpu_custom_call" | custom-call | tf_op jit(solution)/shard_map/hand_over/pallas_call | solution.py:612

commit v7 on v6

--- a/solution.py
+++ b/solution.py
@@ -372,7 +372,7 @@
             def _():
                 z_start(way_a(i + 3))
 
-            @pl.when(i + 4 == WAYS)
+            @pl.when(i + 3 == WAYS)
             def _():
                 for k in range(2):
                     hcopy(k).wait_recv()

time: 68.1 us -> 67.9 us (level)
  no operation moved by 1% of the time
where the time goes in v7:
time: 67.9 us; the launch traced here: 66.9 us
  Pallas kernels  66.3 us (98%)
    pallas_call x1, Pallas kernels, local(): pl.pallas_call(kernel, out_shape=(jax.ShapeDtypeStruct((HEADS, 128), f32)...  64.4 us
    pallas_call x1, Pallas kernels, local(): pl.pallas_call(hand_over, out_shape=[jax.ShapeDtypeStruct(r.shape, r.dtyp...  1.91 us

profile of v7, /device:TPU:2, one launch (start us, length us, event | category | flops | bytes accessed | tf_op | source)
XLA Modules:
  0.0 66.9 jit_solution(1653087103457980045)
XLA Ops:
  0.6 64.4 %fused.1 = (f32[8,128]{1,0:T(8,128)}, bf16[256,8,128]{2,1,0:T(8,128)(2,1)}, bf16[256,128]{1,0:T(8,128)(2,1)}, bf16[256,128]{1,0:T(8,128)(2,1)}) custom-call(bf16[256,8,128]{2,1,0:T(8,128)(2,1)} %bitcast.11, bf16[256,128]{1,0:T(8,128)(2,1)} %bitcast.12, bf16[256,128]{1,0:T(8,128)(2,1)} %bitcast.13, s32[1,256]{1,0:T(1,128)} %seg_ref.1, s32[128,1024]{1,0:T(8,128)} %codes_hbm.1, ...), custom_call_target="tpu_custom_call" | custom-call | tf_op jit(solution)/shard_map/fused/pallas_call | solution.py:558
  65.0 1.9 %hand_over.1 = (f32[8,128]{1,0:T(8,128)}, bf16[256,8,128]{2,1,0:T(8,128)(2,1)}, bf16[256,128]{1,0:T(8,128)(2,1)}, bf16[256,128]{1,0:T(8,128)(2,1)}) custom-call(f32[8,128]{1,0:T(8,128)} %get-tuple-element.12.refs_0_, bf16[256,8,128]{2,1,0:T(8,128)(2,1)} %get-tuple-element.13.refs_1_, bf16[256,128]{1,0:T(8,128)(2,1)} %get-tuple-element.14.refs_2_, ...), custom_call_target="tpu_custom_call" | custom-call | tf_op jit(solution)/shard_map/hand_over/pallas_call | solution.py:612
